TPU v7x, 128 devices: a whole 4x4x4 slice. The times are simulated.
128 devices in a mesh: catalog: 16 (over y_lo, z, core), query: 4 (over x), dp: 2 (over y_hi).
Axes of the slice: x: 4, y: 4 (y_hi: 2, y_lo: 2; y = y_hi * 2 + y_lo), z: 4, core: 2. Of those that a mesh axis runs over, the one named last changes fastest.
Arguments:
- slab: bfloat16 [262144, 512], P('catalog'), may hold values from -6 to 6
- fetch_rows: int32 [16, 16, 512], P('catalog', None, ('query', 'dp')), may hold values from 0 to 16383, as said below
- w_in: bfloat16 [512, 2048], replicated, may hold values from -0.25 to 0.25
- b_in: float32 [2048], replicated, may hold values from -3 to 3
- w_out: bfloat16 [2048, 512], replicated, may hold values from -0.125 to 0.125
- query_emb: bfloat16 [8192, 512], P(('query', 'dp')), may hold values from -2400 to 2400
- item_counts: int32 [16, 16, 512], P('catalog'), may hold values from 1 to 199
- tile_blocks: int32 [64, 16, 8], P(('query', 'dp'), 'catalog'), may hold values from 0 to 63, as said below
- tile_count: int32 [64, 16], P(('query', 'dp'), 'catalog'), may hold values from 1 to 8
- pos_idx: int32 [8192], P(('query', 'dp')), may hold values from 0 to 131071, as said below
Outputs:
- cand_vectors: bfloat16 [16, 16, 512, 512], P('catalog', None, ('query', 'dp'))
- query_loss: float32 [8192], P(('query', 'dp'))
Inputs may be any that keep to these rules, and one draw needn't show every extreme that they name: For each owner o the 8192 entries of fetch_rows[o] are distinct. The entries of tile_blocks[b, t] are distinct. `pos_idx`: each query's positive lies in a block listed for its query block.
All inputs are finite; a program needn't handle non-finite values.
Results may differ from a plain program's by a relative error of at most 0.005.
Values may be sent and summed in bfloat16 or wider, within the bound.
A program may use at most 192 MiB of HBM per device.

v0:
```python
import jax
import jax.numpy as jnp
from jax import lax
from jax.sharding import PartitionSpec as P

BLOCK = 128
LIST = 8


def combined_all(value, axis, join):
    pieces = jax.tree.map(lambda part: lax.all_gather(part, axis), value)
    head = jax.tree.map(lambda part: part[0], pieces)
    tail = jax.tree.map(lambda part: part[1:], pieces)
    subtotal, _ = lax.scan(lambda subtotal, piece: (join(subtotal, piece), None), head, tail)
    return subtotal


def item_tower(item_rows, w_in, b_in, w_out):
    flat_rows = item_rows.reshape(-1, item_rows.shape[-1])
    hidden = jnp.maximum(
        jnp.dot(flat_rows, w_in, preferred_element_type=jnp.float32) + b_in, 0.0
    ).astype(jnp.bfloat16)
    output = jnp.dot(hidden, w_out, preferred_element_type=jnp.float32)
    normed = (output * lax.rsqrt(jnp.sum(output * output, axis=-1, keepdims=True) + 1e-06)).astype(
        jnp.bfloat16
    )
    return normed.reshape(item_rows.shape[:-1] + (w_out.shape[1],))


def combine(left_stats, right_stats):
    peak_score = jnp.maximum(left_stats[0], right_stats[0])
    exp_total = left_stats[1] * jnp.exp(left_stats[0] - peak_score) + right_stats[1] * jnp.exp(
        right_stats[0] - peak_score
    )
    return (peak_score, exp_total, left_stats[2] + right_stats[2])


def column_stats(queries, tile_lists, list_valid, wanted, piece_rows, log_piece, column_ids):
    scores = lax.dot_general(
        queries, piece_rows, (((1,), (1,)), ((), ())), preferred_element_type=jnp.float32
    )
    scores = scores - log_piece[None, :]
    block_ids = column_ids // BLOCK
    member = jnp.any(
        (tile_lists[:, :, None] == block_ids[None, None, :]) & list_valid[:, :, None], axis=1
    )
    block_count = tile_lists.shape[0]
    scores = scores.reshape(block_count, -1, scores.shape[1])
    keep_mask = member[:, None, :]
    peak_score = jnp.max(jnp.where(keep_mask, scores, -1e30), axis=2)
    exp_total = jnp.sum(jnp.where(keep_mask, jnp.exp(scores - peak_score[:, :, None]), 0.0), axis=2)
    match_mask = column_ids[None, None, :] == wanted.reshape(block_count, -1)[:, :, None]
    positive_score = jnp.sum(jnp.where(match_mask, scores, 0.0), axis=2)
    return (peak_score.reshape(-1), exp_total.reshape(-1), positive_score.reshape(-1))


def per_device(
    slab, fetch_rows, w_in, b_in, w_out, query_emb, item_counts, tile_blocks, tile_count, pos_idx
):
    cat_count = lax.axis_size("catalog")
    slot_count = item_counts.shape[2]
    feature_width = slab.shape[1]
    cand_total = cat_count * slot_count
    picked = jnp.take(slab, fetch_rows[0], axis=0)
    own_panel = item_tower(
        lax.all_to_all(picked, "catalog", split_axis=0, concat_axis=0, tiled=True),
        w_in,
        b_in,
        w_out,
    )
    log_counts = jnp.log(item_counts[0].astype(jnp.float32))
    listed = tile_blocks[:, 0, :]
    list_slots = jnp.arange(LIST, dtype=jnp.int32)[None, :]
    valid_mask = list_slots < tile_count
    offset = lax.axis_index("catalog") * cand_total
    owners_base = jnp.arange(cat_count, dtype=jnp.int32)[:, None] * slot_count
    wanted = pos_idx - offset
    query_count = query_emb.shape[0]
    fold_start = (
        jnp.full((query_count,), -1e30, jnp.float32),
        jnp.zeros((query_count,), jnp.float32),
        jnp.zeros((query_count,), jnp.float32),
    )
    piece = lax.all_gather(own_panel, ("query", "dp"), axis=1, tiled=True)
    piece_width = piece.shape[1]
    column_ids = (owners_base + jnp.arange(piece_width, dtype=jnp.int32)[None, :]).reshape(-1)
    log_piece = log_counts.reshape(-1)
    softmax_stats = combine(
        fold_start,
        column_stats(
            query_emb,
            listed,
            valid_mask,
            wanted,
            piece.reshape(-1, feature_width),
            log_piece,
            column_ids,
        ),
    )
    merged = combined_all(softmax_stats, "catalog", combine)
    query_loss = merged[0] + jnp.log(merged[1]) - merged[2]
    return (own_panel[None], query_loss)


def solution(mesh):
    in_specs = (
        P("catalog", None),
        P("catalog", None, ("query", "dp")),
        P(),
        P(),
        P(),
        P(("query", "dp"), None),
        P("catalog", None, None),
        P(("query", "dp"), "catalog", None),
        P(("query", "dp"), "catalog"),
        P(("query", "dp")),
    )
    out_specs = (P("catalog", None, ("query", "dp"), None), P(("query", "dp")))
    return jax.shard_map(
        per_device, mesh=mesh, in_specs=in_specs, out_specs=out_specs, check_vma=False
    )
```

profile of v0, /device:TPU:1, one launch (start us, length us, event | category | flops | bytes accessed | tf_op | source)
XLA Modules:
  0.0 290.3 jit_solution(5409098877619454827)
XLA Ops:
  7.2 0.0 copy-start
  7.2 0.0 copy-start.6
  7.2 0.0 all-gather.5.cloned.1.call-start
  7.2 0.8 compare_select_fusion
  8.1 0.7 compare_and_fusion
  8.8 0.1 reshape.189
  8.9 11.9 %gather_fusion = bf16[1024,512]{1,0:T(8,128)(2,1)S(1)} fusion(bf16[16384,512]{1,0:T(8,128)(2,1)} %param.12, s32[1024]{0:T(1024)S(1)} %broadcast_clamp_fusion), kind=kCustom, calls=%fused_computation | custom fusion | bytes 2101248 | tf_op jit(solution)/shard_map/jit(_take)/gather | solution.py:64
  20.8 0.2 broadcast_select_fusion
  21.0 23.1 %all_to_all.5 = bf16[16,64,512]{2,1,0:T(8,128)(2,1)S(1)} all-to-all(bf16[16,64,512]{2,1,0:T(8,128)(2,1)S(1)} %broadcast_select_fusion), channel_id=1, replica_groups=mesh['catalog'=16,'query'=4,'dp'=2] {'catalog'}, dimensions={0} | all-to-all | bytes 2097152 | tf_op jit(solution)/shard_map/all_to_all | solution.py:66
  44.0 0.0 copy-done
  44.1 0.0 copy-done.6
  44.1 0.0 copy-start.2
  44.1 0.0 copy-start.4
  44.1 7.5 %multiply_reduce_fusion = (f32[1024]{0:T(1024)S(1)}, f32[1024,512]{1,0:T(8,128)}) fusion(bf16[2048,512]{1,0:T(8,128)(2,1)S(1)} %copy-done, f32[2048]{0:T(1024)S(1)} %copy-done.6, bf16[1024,512]{1,0:T(8,128)(2,1)S(1)} %bitcast.74, bf16[512,2048]{1,0:T(8,128)(2,1)} %param.14), kind=kOutput, calls=%fused_computation.18 | convolution fusion | flops 4302306304 | bytes 7352320 | tf_op jit(solution)/shard_map/dot_general | solution.py:23
  51.5 2.8 multiply_convert_fusion
  54.3 0.0 all-gather.5.cloned.1.call-update
  54.4 0.1 add_bitcast_fusion
  54.4 0.0 copy-done.7
  54.5 0.1 iota_compare_fusion
  54.6 0.8 and_reduce_fusion
  55.4 1.7 copy.12
  57.1 0.0 copy-start.5
  57.2 0.0 copy-done.4
  57.2 105.2 %all-gather.5.cloned.1.call-done = bf16[16,512,512]{2,1,0:T(8,128)(2,1)} async-done(((bf16[16,64,512]{2,1,0:T(8,128)(2,1)}), bf16[16,512,512]{2,1,0:T(8,128)(2,1)}) %all-gather.5.cloned.1.call-update) | async-done | bytes 8388624 | tf_op jit(solution)/shard_map/all_gather | solution.py:84
  162.4 25.1 %broadcast_in_dim.49 = pred[8,128,8192]{1,0,2:T(8,128)(4,1)} broadcast(pred[8,8192]{0,1:T(8,128)(4,1)S(1)} %copy.12), dimensions={0,2} | broadcast | bytes 8454144 | tf_op jit(solution)/shard_map/jit(_where)/broadcast_in_dim | solution.py:50
  187.5 20.8 %fusion = (f32[1024]{0:T(1024)S(1)}, f32[8192,1024]{1,0:T(8,128)}) fusion(pred[1024,8,8,128]{3,2,1,0:T(8,128)(4,1)} %bitcast.69, f32[8192]{0:T(1024)S(1)} %bitcast.82, bf16[8192,512]{1,0:T(8,128)(2,1)} %bitcast.89, bf16[1024,512]{1,0:T(8,128)(2,1)S(1)} %copy-done.5), kind=kOutput, calls=%fused_computation.8 | convolution fusion | flops 8615099392 | bytes 51417088 | tf_op jit(solution)/shard_map/dot_general | solution.py:39
  208.3 18.8 %fusion.4 = (f32[1024]{0:T(1024)S(1)}, f32[1024]{0:T(1024)S(1)}) fusion(f32[8192,1024]{1,0:T(8,128)} %get-tuple-element.69, s32[1024]{0:T(1024)S(1)} %broadcast_subtract_fusion, f32[8192]{0:T(1024)S(1)} %bitcast.83, s32[8192]{0:T(1024)S(1)} %bitcast.79, f32[1024]{0:T(1024)S(1)} %get-tuple-element.68, pred[1024,8,8,128]{3,2,1,0:T(8,128)(4,1)} %bitcast.70), kind=kLoop, calls=%fused_computation.12 | loop fusion | flops 58718208 | bytes 42024960 | tf_op jit(solution)/shard_map/reduce_sum | solution.py:53
  227.2 20.0 %all-gather.1 = f32[16,1,1024]{2,1,0:T(1,128)S(1)} all-gather(f32[1,1,1024]{2,1,0:T(1,128)S(1)} %get-tuple-element.65), channel_id=1, replica_groups=mesh['catalog'=16,'query'=4,'dp'=2] {'catalog'}, dimensions={0}, use_global_device_ids=true | all-gather | bytes 69632 | tf_op jit(solution)/shard_map/all_gather | solution.py:11
  247.2 16.4 %all-gather.2 = f32[16,1,1024]{2,1,0:T(1,128)S(1)} all-gather(f32[1,1,1024]{2,1,0:T(1,128)S(1)} %get-tuple-element.64), channel_id=1, replica_groups=mesh['catalog'=16,'query'=4,'dp'=2] {'catalog'}, dimensions={0}, use_global_device_ids=true | all-gather | bytes 69632 | tf_op jit(solution)/shard_map/all_gather | solution.py:11
  263.7 17.7 %all-gather = f32[16384]{0:T(1024)S(1)} all-gather(f32[1024]{0:T(1024)S(1)} %get-tuple-element.44), channel_id=2, replica_groups=mesh['catalog'=16,'query'=4,'dp'=2] {'catalog'}, dimensions={0}, use_global_device_ids=true | all-gather | bytes 69632 | tf_op jit(solution)/shard_map/all_gather | solution.py:11
  281.5 1.3 while.14
  282.8 0.6 add_subtract_fusion
  (85 shorter events, 0.8 us)
Async XLA Ops:
  7.2 36.9 %copy-start = (bf16[2048,512]{1,0:T(8,128)(2,1)S(1)}, bf16[2048,512]{1,0:T(8,128)(2,1)}, u32[]{:S(2)}) copy-start(bf16[2048,512]{1,0:T(8,128)(2,1)} %param.16) | copy-start | bytes 6291460
  7.2 36.9 %copy-start.6 = (f32[2048]{0:T(1024)S(1)}, f32[2048]{0:T(1024)}, u32[]{:S(2)}) copy-start(f32[2048]{0:T(1024)} %param.15) | copy-start | bytes 24580
  7.2 155.2 %all-gather.5.cloned.1.call-start = ((), (), s32[]{:S(2)}) async-start(), calls=%async_computation.1 | async-start | bytes 9437184 | tf_op jit(solution)/shard_map/all_gather | solution.py:84
  44.1 10.4 %copy-start.7 = (s32[8,1]{0,1:T(1,128)S(1)}, s32[8,1]{0,1:T(1,128)}, u32[]{:S(2)}) copy-start(s32[8,1]{0,1:T(1,128)} %param.20) | copy-start | bytes 100
  44.1 10.5 %copy-start.3 = (s32[8,1,8]{2,1,0:T(1,128)S(1)}, s32[8,1,8]{2,1,0:T(1,128)}, u32[]{:S(2)}) copy-start(s32[8,1,8]{2,1,0:T(1,128)} %param.19) | copy-start | bytes 772
  44.1 13.0 %copy-start.2 = (s32[1,16,512]{2,1,0:T(8,128)S(1)}, s32[1,16,512]{2,1,0:T(8,128)}, u32[]{:S(2)}) copy-start(s32[1,16,512]{2,1,0:T(8,128)} %param.18) | copy-start | bytes 98308
  44.1 13.1 %copy-start.4 = (s32[1024]{0:T(1024)S(1)}, s32[1024]{0:T(1024)}, u32[]{:S(2)}) copy-start(s32[1024]{0:T(1024)} %param.21) | copy-start | bytes 12292
  57.1 130.4 %copy-start.5 = (bf16[1024,512]{1,0:T(8,128)(2,1)S(1)}, bf16[1024,512]{1,0:T(8,128)(2,1)}, u32[]{:S(2)}) copy-start(bf16[1024,512]{1,0:T(8,128)(2,1)} %param.17) | copy-start | bytes 3145732
  208.3 75.1 %copy-start.1 = (bf16[2048,512]{1,0:T(8,128)(2,1)S(1)}, bf16[2048,512]{1,0:T(8,128)(2,1)}, u32[]{:S(2)}) copy-start(bf16[2048,512]{1,0:T(8,128)(2,1)} %param.16) | copy-start | bytes 6291460
Sparse Core Ops, SparseCore 0:
  54.5 107.9 all-gather.4
where the time goes:
time: 291 us; the launch traced here: 290 us
  waiting for transfers between devices  105 us (36%)
  blocking collectives  77.2 us (27%)
  local copies, waits for them, and re-layouts  39.3 us (14%)
  matrix products  28.3 us (10%)
  other arithmetic  25.3 us (9%)
  between operations  14.2 us (5%)
    all_gather x1, waiting for transfers between devices, per_device(): piece = lax.all_gather(own_panel, ('query', 'dp'), axis=1, tiled=True)  105 us
    all_gather x3, blocking collectives, combined_all(): pieces = jax.tree.map(lambda part: lax.all_gather(part, axis), value)  54.2 us
    broadcast_in_dim x1, local copies, waits for them, and re-layouts, column_stats(): peak_score = jnp.max(jnp.where(keep_mask, scores, -1e+30), axis=2)  25.1 us
    all_to_all x1, blocking collectives, per_device(): lax.all_to_all(picked, 'catalog', split_axis=0, concat_axis=0, tiled=True)  23.1 us
    dot_general x1, matrix products, column_stats(): lax.dot_general(queries, piece_rows, (((1,), (1,)), ((), ())), preferred_...  20.8 us
    reduce_sum x1, other arithmetic, column_stats(): positive_score = jnp.sum(jnp.where(match_mask, scores, 0.0), axis=2)  18.8 us
    gather x1, local copies, waits for them, and re-layouts, per_device(): picked = jnp.take(slab, fetch_rows[0], axis=0)  11.9 us
    dot_general x1, matrix products, item_tower(): output = jnp.dot(hidden, w_out, preferred_element_type=jnp.float32)  7.46 us
  transfers between devices with their start and end apart: 1, of which 1 were waited for; matrix products, arithmetic and copies ran while one was open for 1% of the time, Pallas kernels for 0%

commit v1 on v0

v1 whole, which is shorter than its diff:
```python
import functools

import jax
import jax.numpy as jnp
from jax import lax
from jax.experimental import pallas as pl
from jax.experimental.pallas import tpu as pltpu
from jax.sharding import PartitionSpec as P

MESH = pl.DeviceIdType.MESH
ANY = pl.BlockSpec(memory_space=pl.ANY)
VMEM = pl.BlockSpec(memory_space=pltpu.VMEM)
SMEM = pl.BlockSpec(memory_space=pltpu.SMEM)

E = 512
H = 2048
NC = 16
NX = 4
ND = 2
NJ = NX * ND
SUB = 64
LIST = 8
ROWS = 16384
QROWS = 1024
QB = QROWS // 128
HALF = QROWS // 2
SLAB_CHUNK = 1024
JOBS = 4
LOW = -1e30


def flip(value, bits, width):
    out = value
    for bit in range(width):
        if (bits >> bit) & 1:
            out = out + (1 << bit) * (1 - 2 * ((value // (1 << bit)) % 2))
    return out


FLOWS = (
    ("y", (0, 0), 0, 256, None),
    ("r", (0, 0), 0, 256, None),
    ("l", (0, 0), 256, 256, None),
    ("y", (0, 0), 256, 256, None),
    ("r", (0, 0), 256, 256, None),
    ("l", (0, 0), 0, 256, None),
    ("r", (-1, 0), 0, 256, 1),
    ("l", (1, 0), 256, 256, 2),
    ("r", (0, 1), 0, 256, 0),
    ("l", (0, 1), 0, 256, 0),
    ("y", (1, 0), 256, 256, 2),
    ("y", (-1, 0), 256, 256, 4),
    ("y", (2, 0), 256, 256, 7),
    ("r", (-1, 1), 0, 128, 8),
    ("l", (1, 1), 128, 128, 9),
)


def landed(flow):
    hop, (ox, oy), *_ = FLOWS[flow]
    return {"r": (ox - 1, oy), "l": (ox + 1, oy), "y": (ox, 1 - oy)}[hop]


def tower_kernel(
    fetch, slab, query, pos, lists, counts, w_in, b_in, w_out,
    queries, meta_all, cand_out,
    chunk, table, rowbuf, staged, arrived, meta, w_in_v, w_out_v, cand,
    slab_sem, w_sem, own_sem, meta_send, meta_recv, a2a_send, a2a_recv, flow_send, flow_recv, core_send, core_recv, out_sem,
):
    t = lax.axis_index("catalog")
    x = lax.axis_index("query")
    d = lax.axis_index("dp")
    core = t % 2
    j = x * ND + d

    n_chunks = ROWS // SLAB_CHUNK
    depth = chunk.shape[0]

    def slab_copy(n):
        slot = n % depth
        rows = pl.ds(pl.multiple_of(n * SLAB_CHUNK, SLAB_CHUNK), SLAB_CHUNK)
        return pltpu.make_async_copy(slab.at[rows], chunk.at[slot], slab_sem.at[slot])

    for n in range(depth):
        slab_copy(n).start()

    meta_peers = [(dx, dd) for dx in range(NX) for dd in range(ND) if (dx, dd) != (0, 0)]
    right, left = (x + 1) % NX, (x + NX - 1) % NX
    hop_to = {
        "r": {"catalog": t, "query": right, "dp": d},
        "l": {"catalog": t, "query": left, "dp": d},
        "y": {"catalog": flip(t, 8, 4), "query": x, "dp": 1 - d},
    }
    sibling = {"catalog": flip(t, 1, 4), "query": x, "dp": d}

    barrier = pltpu.get_barrier_semaphore()
    n_peers = 0
    for k in range(1, NC):
        pl.semaphore_signal(barrier, inc=1, device_id={"catalog": flip(t, k, 4), "query": x, "dp": d}, device_id_type=MESH)
        n_peers += 1
    for dx, dd in meta_peers:
        pl.semaphore_signal(
            barrier, inc=1, device_id={"catalog": t, "query": (x + dx) % NX, "dp": (d + dd) % ND}, device_id_type=MESH
        )
        n_peers += 1
    pl.semaphore_signal(barrier, inc=1, device_id=hop_to["y"], device_id_type=MESH)
    n_peers += 1

    meta[...] = jnp.zeros_like(meta)
    meta[0:QB, :] = pos[...]
    meta[QB : 2 * QB, 0:LIST] = lists[:, 0, :]
    meta[QB : 2 * QB, LIST : LIST + 1] = counts[...]
    pl.semaphore_wait(barrier, n_peers)

    def origin(place):
        ox, oy = place
        xo = (x + ox + NX) % NX
        return xo * ND + (1 - d if oy else d)

    def flow_copy(n):
        hop, place, first, count, _ = FLOWS[n]
        jo = origin(place)
        rows = pl.ds(pl.multiple_of(core * HALF + first, 128), count)
        src = query.at[rows] if place == (0, 0) else queries.at[jo, rows]
        return pltpu.make_async_remote_copy(
            src_ref=src,
            dst_ref=queries.at[jo, rows],
            send_sem=flow_send.at[n],
            recv_sem=flow_recv.at[n],
            device_id=hop_to[hop],
            device_id_type=MESH,
        )

    def core_copy(n):
        _, _, first, count, _ = FLOWS[n]
        jo = origin(landed(n))
        rows = pl.ds(pl.multiple_of(core * HALF + first, 128), count)
        return pltpu.make_async_remote_copy(
            src_ref=queries.at[jo, rows],
            dst_ref=queries.at[jo, rows],
            send_sem=core_send.at[n],
            recv_sem=core_recv.at[n],
            device_id=sibling,
            device_id_type=MESH,
        )

    def advance(flows):
        for n in flows:
            flow_copy(n).wait_recv()
            for later, flow in enumerate(FLOWS):
                if flow[4] == n:
                    flow_copy(later).start()
            core_copy(n).start()

    for n, flow in enumerate(FLOWS):
        if flow[4] is None:
            flow_copy(n).start()

    def meta_copy(n):
        dx, dd = meta_peers[n]
        return pltpu.make_async_remote_copy(
            src_ref=meta,
            dst_ref=meta_all.at[j],
            send_sem=meta_send.at[n],
            recv_sem=meta_recv.at[n],
            device_id={"catalog": t, "query": (x + dx) % NX, "dp": (d + dd) % ND},
            device_id_type=MESH,
        )

    for n in range(len(meta_peers)):
        meta_copy(n).start()
    own_query = pltpu.make_async_copy(query, queries.at[j], own_sem.at[0])
    own_meta = pltpu.make_async_copy(meta, meta_all.at[j], own_sem.at[1])
    own_query.start()
    own_meta.start()

    @pl.loop(0, n_chunks)
    def _(n):
        slot = n % depth
        slab_copy(n).wait()

        @pl.loop(0, SLAB_CHUNK // 64)
        def _(i):
            rows = pl.ds(pl.multiple_of(i * 64, 64), 64)
            to = pl.ds(pl.multiple_of(n * SLAB_CHUNK + i * 64, 64), 64)
            table[to, :] = chunk[slot, rows, :].astype(jnp.float32)

        @pl.when(n + depth < n_chunks)
        def _():
            slab_copy(n + depth).start()

    w_in_copy = pltpu.make_async_copy(w_in, w_in_v, w_sem.at[0])
    w_out_copy = pltpu.make_async_copy(w_out, w_out_v, w_sem.at[1])
    w_in_copy.start()
    w_out_copy.start()

    def a2a_copy(k):
        to = flip(t, k, 4)
        return pltpu.make_async_remote_copy(
            src_ref=staged.at[k],
            dst_ref=arrived.at[t],
            send_sem=a2a_send.at[k],
            recv_sem=a2a_recv.at[k],
            device_id={"catalog": to, "query": x, "dp": d},
            device_id_type=MESH,
        )

    for k in range(NC - 1, -1, -1):
        to = flip(t, k, 4)

        @pl.loop(0, SUB // 16)
        def _(i):
            for u in range(16):
                row = fetch[0, to, i * 16 + u]
                rowbuf[pl.ds(i * 16 + u, 1), :] = table[pl.ds(row, 1), :]

        if k:
            staged[k] = rowbuf[...].astype(jnp.bfloat16)
            a2a_copy(k).start()
        else:
            arrived[t] = rowbuf[...].astype(jnp.bfloat16)

    advance((0, 1, 2))
    w_in_copy.wait()
    w_out_copy.wait()

    def tower(group):
        base = 4 * flip(t // 4, group, 2)
        for k in range(4 * group, 4 * group + 4):
            if k:
                a2a_copy(k).wait_recv()
        rows = arrived[pl.ds(base, 4)].reshape(4 * SUB, E)
        hidden = jnp.maximum(jnp.dot(rows, w_in_v[...], preferred_element_type=jnp.float32) + b_in[...], 0.0).astype(jnp.bfloat16)
        y = jnp.dot(hidden, w_out_v[...], preferred_element_type=jnp.float32)
        normed = y * lax.rsqrt(jnp.sum(y * y, axis=-1, keepdims=True) + 1e-06)
        cand[pl.ds(base, 4)] = normed.astype(jnp.bfloat16).reshape(4, SUB, E)
        pltpu.make_async_copy(cand.at[pl.ds(base, 4)], cand_out.at[pl.ds(base, 4)], out_sem.at[group]).start()

    tower(0)
    advance((3, 4, 5))
    tower(1)
    advance((7, 6, 8, 9))
    tower(2)
    tower(3)
    advance((10, 11, 12, 13, 14))

    for group in range(4):
        base = 4 * flip(t // 4, group, 2)
        pltpu.make_async_copy(cand.at[pl.ds(base, 4)], cand_out.at[pl.ds(base, 4)], out_sem.at[group]).wait()
    for k in range(1, NC):
        a2a_copy(k).wait_send()
    for n in range(len(FLOWS)):
        flow_copy(n).wait_send()
        core_copy(n).wait()
    for n in range(len(meta_peers)):
        meta_copy(n).wait()
    own_query.wait()
    own_meta.wait()


def run_tower(fetch, slab, query, pos, lists, counts, w_in, b_in, w_out):
    dma = pltpu.SemaphoreType.DMA
    return pl.pallas_call(
        tower_kernel,
        out_shape=(
            jax.ShapeDtypeStruct((NJ, QROWS, E), jnp.bfloat16),
            jax.ShapeDtypeStruct((NJ, 2 * QB, 128), jnp.int32),
            jax.ShapeDtypeStruct((NC, SUB, E), jnp.bfloat16),
        ),
        in_specs=[SMEM, ANY, ANY, VMEM, VMEM, VMEM, ANY, VMEM, ANY],
        out_specs=(ANY, ANY, ANY),
        scratch_shapes=[
            pltpu.VMEM((4, SLAB_CHUNK, E), jnp.bfloat16),
            pltpu.VMEM((ROWS, E), jnp.float32),
            pltpu.VMEM((SUB, E), jnp.float32),
            pltpu.VMEM((NC, SUB, E), jnp.bfloat16),
            pltpu.VMEM((NC, SUB, E), jnp.bfloat16),
            pltpu.VMEM((2 * QB, 128), jnp.int32),
            pltpu.VMEM((E, H), jnp.bfloat16),
            pltpu.VMEM((H, E), jnp.bfloat16),
            pltpu.VMEM((NC, SUB, E), jnp.bfloat16),
            dma((4,)),
            dma((2,)),
            dma((2,)),
            dma((NJ - 1,)),
            dma((NJ - 1,)),
            dma((NC,)),
            dma((NC,)),
            dma((len(FLOWS),)),
            dma((len(FLOWS),)),
            dma((len(FLOWS),)),
            dma((len(FLOWS),)),
            dma((4,)),
        ],
        compiler_params=pltpu.CompilerParams(
            collective_id=0, has_side_effects=True, vmem_limit_bytes=58 * 1024 * 1024
        ),
        cost_estimate=pl.CostEstimate(flops=4 * 1024 * E * H, bytes_accessed=32 << 20, transcendentals=0),
        name="tower",
    )(fetch, slab, query, pos, lists, counts, w_in, b_in, w_out)


def score_kernel(
    queries, meta_all, cand_in, item_counts,
    stats, cand_out,
    q, meta_s, meta_v, cand, logt, neg_log, jobs, top, total, positive,
    q_sem, sem,
):
    t = lax.axis_index("catalog")
    x = lax.axis_index("query")
    d = lax.axis_index("dp")
    j = x * ND + d

    to_smem = pltpu.make_async_copy(meta_all, meta_s, sem.at[0])
    to_vmem = pltpu.make_async_copy(meta_all, meta_v, sem.at[1])
    cand_load = pltpu.make_async_copy(cand_in, cand, sem.at[2])
    cand_store = pltpu.make_async_copy(cand, cand_out, sem.at[3])
    to_smem.start()
    to_vmem.start()
    cand_load.start()
    q_loads = [pltpu.make_async_copy(queries.at[n], q.at[pl.ds(n * QROWS, QROWS)], q_sem.at[n]) for n in range(NJ)]
    for load in q_loads:
        load.start()

    top[...] = jnp.full_like(top, LOW)
    total[...] = jnp.zeros_like(total)
    positive[...] = jnp.zeros_like(positive)
    logt[...] = jnp.transpose(-jnp.log(item_counts[...].astype(jnp.float32)))
    own = logt[pl.ds(pl.multiple_of(j * SUB, SUB), SUB), :]
    for o in range(NC):
        neg_log[o] = jnp.broadcast_to(own[:, o : o + 1], (SUB, 128))

    to_smem.wait()

    def list_block(b, n):
        count = meta_s[b // QB, QB + b % QB, LIST]
        for e in range(LIST):
            block = meta_s[b // QB, QB + b % QB, e]
            jobs[n] = b * NC + block // 4
            n = n + jnp.where((e < count) & (block % 4 == x), 1, 0)
        return n

    n_jobs = lax.fori_loop(0, NJ * QB, list_block, jnp.int32(0))
    for u in range(JOBS):
        jobs[n_jobs + u] = NJ * QB * NC
    to_vmem.wait()
    cand_load.wait()
    cand_store.start()
    for load in q_loads:
        load.wait()

    row_ids = lax.broadcasted_iota(jnp.int32, (SUB, 128), 0)

    @pl.loop(0, (n_jobs + JOBS - 1) // JOBS)
    def _(step):
        found = []
        for u in range(JOBS):
            job = jobs[step * JOBS + u]
            b, o = job // NC, job % NC
            b_q = jnp.minimum(b, NJ * QB - 1)
            block = q[pl.ds(pl.multiple_of(b_q * 128, 128), 128), :]
            scores = lax.dot_general(cand[o], block, (((1,), (1,)), ((), ())), preferred_element_type=jnp.float32)
            scores = scores + neg_log[o]
            wanted = meta_v[b_q // QB, pl.ds(b_q % QB, 1), :] - (t * (NC * 512) + o * 512 + j * SUB)
            peak = jnp.max(scores, axis=0, keepdims=True)
            mass = jnp.sum(jnp.exp(scores - peak), axis=0, keepdims=True)
            match = jnp.sum(jnp.where(row_ids == wanted, scores, 0.0), axis=0, keepdims=True)
            found.append((b, peak, mass, match))
        for b, peak, mass, match in found:
            at = pl.ds(b, 1)
            old = top[at, :]
            new = jnp.maximum(old, peak)
            total[at, :] = total[at, :] * jnp.exp(old - new) + mass * jnp.exp(peak - new)
            positive[at, :] = positive[at, :] + match
            top[at, :] = new

    for n in range(NJ):
        stats[n, 0:QB, :] = top[n * QB : (n + 1) * QB, :]
        stats[n, QB : 2 * QB, :] = total[n * QB : (n + 1) * QB, :]
        stats[n, 2 * QB : 3 * QB, :] = positive[n * QB : (n + 1) * QB, :]
    cand_store.wait()


def run_score(queries, meta_all, cand, item_counts):
    dma = pltpu.SemaphoreType.DMA
    return pl.pallas_call(
        score_kernel,
        out_shape=(
            jax.ShapeDtypeStruct((NJ, 3 * QB, 128), jnp.float32),
            jax.ShapeDtypeStruct((NC, SUB, E), jnp.bfloat16),
        ),
        in_specs=[ANY, ANY, ANY, VMEM],
        out_specs=(VMEM, ANY),
        scratch_shapes=[
            pltpu.VMEM((NJ * QROWS, E), jnp.bfloat16),
            pltpu.SMEM((NJ, 2 * QB, 128), jnp.int32),
            pltpu.VMEM((NJ, 2 * QB, 128), jnp.int32),
            pltpu.VMEM((NC, SUB, E), jnp.bfloat16),
            pltpu.VMEM((512, NC), jnp.float32),
            pltpu.VMEM((NC, SUB, 128), jnp.float32),
            pltpu.SMEM((NJ * QB * LIST + 2 * JOBS,), jnp.int32),
            pltpu.VMEM((NJ * QB + 8, 128), jnp.float32),
            pltpu.VMEM((NJ * QB + 8, 128), jnp.float32),
            pltpu.VMEM((NJ * QB + 8, 128), jnp.float32),
            dma((NJ,)),
            dma((4,)),
        ],
        compiler_params=pltpu.CompilerParams(vmem_limit_bytes=58 * 1024 * 1024),
        cost_estimate=pl.CostEstimate(flops=1 << 29, bytes_accessed=10 << 20, transcendentals=1 << 20),
        name="score",
    )(queries, meta_all, cand, item_counts)


def merged(parts):
    tops = [part[0] for part in parts]
    top = functools.reduce(jnp.maximum, tops)
    total = functools.reduce(jnp.add, [part[1] * jnp.exp(part[0] - top) for part in parts])
    positive = functools.reduce(jnp.add, [part[2] for part in parts])
    return top, total, positive


def thirds(ref, index):
    return tuple(ref[index, n * QB : (n + 1) * QB, :] for n in range(3))


def merge_kernel(stats, loss, by_group, part, by_catalog, send_a, recv_a, send_b, recv_b):
    t = lax.axis_index("catalog")
    x = lax.axis_index("query")
    d = lax.axis_index("dp")
    j = x * ND + d
    peers = [(dx, dd) for dx in range(NX) for dd in range(ND) if (dx, dd) != (0, 0)]

    def group_peer(n):
        dx, dd = peers[n]
        return (x + dx) % NX, (d + dd) % ND

    barrier = pltpu.get_barrier_semaphore()
    for n in range(NJ - 1):
        xp, dp = group_peer(n)
        pl.semaphore_signal(barrier, inc=1, device_id={"catalog": t, "query": xp, "dp": dp}, device_id_type=MESH)
    for k in range(1, NC):
        pl.semaphore_signal(barrier, inc=1, device_id={"catalog": flip(t, k, 4), "query": x, "dp": d}, device_id_type=MESH)
    pl.semaphore_wait(barrier, NJ - 1 + NC - 1)

    def group_copy(n):
        xp, dp = group_peer(n)
        return pltpu.make_async_remote_copy(
            src_ref=stats.at[xp * ND + dp],
            dst_ref=by_group.at[j],
            send_sem=send_a.at[n],
            recv_sem=recv_a.at[n],
            device_id={"catalog": t, "query": xp, "dp": dp},
            device_id_type=MESH,
        )

    for n in range(NJ - 1):
        group_copy(n).start()
    by_group[j] = stats[j]
    for n in range(NJ - 1):
        group_copy(n).wait_recv()
    for n, value in enumerate(merged([thirds(by_group, i) for i in range(NJ)])):
        part[n * QB : (n + 1) * QB, :] = value

    def catalog_copy(k):
        return pltpu.make_async_remote_copy(
            src_ref=part,
            dst_ref=by_catalog.at[t],
            send_sem=send_b.at[k],
            recv_sem=recv_b.at[k],
            device_id={"catalog": flip(t, k, 4), "query": x, "dp": d},
            device_id_type=MESH,
        )

    for k in range(NC - 1, 0, -1):
        catalog_copy(k).start()
    by_catalog[t] = part[...]
    for k in range(NC - 1, 0, -1):
        catalog_copy(k).wait_recv()
    top, total, positive = merged([thirds(by_catalog, i) for i in range(NC)])
    loss[...] = top + jnp.log(total) - positive
    for n in range(NJ - 1):
        group_copy(n).wait_send()
    for k in range(1, NC):
        catalog_copy(k).wait_send()


def run_merge(stats):
    dma = pltpu.SemaphoreType.DMA
    return pl.pallas_call(
        merge_kernel,
        out_shape=jax.ShapeDtypeStruct((QB, 128), jnp.float32),
        in_specs=[VMEM],
        out_specs=VMEM,
        scratch_shapes=[
            pltpu.VMEM((NJ, 3 * QB, 128), jnp.float32),
            pltpu.VMEM((3 * QB, 128), jnp.float32),
            pltpu.VMEM((NC, 3 * QB, 128), jnp.float32),
            dma((NJ - 1,)),
            dma((NJ - 1,)),
            dma((NC,)),
            dma((NC,)),
        ],
        compiler_params=pltpu.CompilerParams(collective_id=1, has_side_effects=True, vmem_limit_bytes=16 * 1024 * 1024),
        name="merge",
    )(stats)


def per_device(
    slab, fetch_rows, w_in, b_in, w_out, query_emb, item_counts, tile_blocks, tile_count, pos_idx
):
    queries, meta_all, cand = run_tower(
        fetch_rows, slab, query_emb, pos_idx.reshape(QB, 128), tile_blocks, tile_count, w_in, b_in.reshape(1, H), w_out
    )
    stats, cand = run_score(queries, meta_all, cand, item_counts.reshape(NC, 512))
    loss = run_merge(stats)
    return (cand[None], loss.reshape(QROWS))


def solution(mesh):
    in_specs = (
        P("catalog", None),
        P("catalog", None, ("query", "dp")),
        P(),
        P(),
        P(),
        P(("query", "dp"), None),
        P("catalog", None, None),
        P(("query", "dp"), "catalog", None),
        P(("query", "dp"), "catalog"),
        P(("query", "dp")),
    )
    out_specs = (P("catalog", None, ("query", "dp"), None), P(("query", "dp")))
    return jax.shard_map(
        per_device, mesh=mesh, in_specs=in_specs, out_specs=out_specs, check_vma=False
    )
```

time: 291 us -> 80.4 us (0.28)
  waiting for transfers between devices: 105 us -> 0 us
  blocking collectives: 77.2 us -> 0 us
  Pallas kernels: 0 us -> 76.6 us
  local copies, waits for them, and re-layouts: 39.3 us -> 2.8 us
  matrix products: 28.3 us -> 0 us
  other arithmetic: 25.3 us -> 0 us
  between operations: 14.2 us -> 0.66 us
    all_gather x1 -> x0, waiting for transfers between devices: 105 us -> none  [per_device(): piece = lax.all_gather(own_panel, ('query', 'dp'), axis=1, tiled=True)]
    pallas_call x0 -> x3, Pallas kernels: none -> 76.6 us  [the longest x1 48.9 us: run_tower(): pl.pallas_call(tower_kernel, out_shape=(jax.ShapeDtypeStruct((NJ, QROWS,...]
    all_gather x3 -> x0, blocking collectives: 54.2 us -> none  [combined_all(): pieces = jax.tree.map(lambda part: lax.all_gather(part, axis), value)]
    dot_general x2 -> x0, matrix products: 28.3 us -> none  [the longest x1 20.8 us: column_stats(): lax.dot_general(queries, piece_rows, (((1,), (1,)), ((), ())), preferred_...]
    broadcast_in_dim x1 -> x0, local copies, waits for them, and re-layouts: 25.1 us -> none  [column_stats(): peak_score = jnp.max(jnp.where(keep_mask, scores, -1e+30), axis=2)]
    all_to_all x1 -> x0, blocking collectives: 23.1 us -> none  [per_device(): lax.all_to_all(picked, 'catalog', split_axis=0, concat_axis=0, tiled=True)]
    reduce_sum x1 -> x0, other arithmetic: 18.8 us -> none  [column_stats(): positive_score = jnp.sum(jnp.where(match_mask, scores, 0.0), axis=2)]
    gather x1 -> x0, local copies, waits for them, and re-layouts: 11.9 us -> none  [per_device(): picked = jnp.take(slab, fetch_rows[0], axis=0)]
  transfers between devices with their start and end apart: 1 -> 0, of which waited for: 1 -> 0; matrix products, arithmetic and copies ran while one was open for 1% -> 0% of each run, Pallas kernels for 0% -> 0%
where the time goes in v1:
time: 80.4 us; the launch traced here: 80.1 us
  Pallas kernels  76.6 us (95%)
  local copies, waits for them, and re-layouts  2.8 us (3%)
    pallas_call x1, Pallas kernels, run_tower(): pl.pallas_call(tower_kernel, out_shape=(jax.ShapeDtypeStruct((NJ, QROWS,...  48.9 us
    pallas_call x1, Pallas kernels, run_merge(): pl.pallas_call(merge_kernel, out_shape=jax.ShapeDtypeStruct((QB, 128), jn...  14.4 us
    pallas_call x1, Pallas kernels, run_score(): pl.pallas_call(score_kernel, out_shape=(jax.ShapeDtypeStruct((NJ, 3 * QB,...  13.3 us
    unnamed x4, local copies, waits for them, and re-layouts  2.8 us

profile of v1, /device:TPU:1, one launch (start us, length us, event | category | flops | bytes accessed | tf_op | source)
XLA Modules:
  0.0 80.1 jit_solution(10300055640660994394)
XLA Ops:
  0.6 1.3 %copy.12.counts = s32[8,1]{1,0:T(8,128)} copy(s32[8,1]{0,1:T(1,128)} %param.18) | data formatting | bytes 64 | tf_op args[8]
  2.0 48.9 %tower.1 = (bf16[8,1024,512]{2,1,0:T(8,128)(2,1)}, s32[8,16,128]{2,1,0:T(8,128)}, bf16[16,64,512]{2,1,0:T(8,128)(2,1)}) custom-call(s32[1,16,64]{2,1,0:T(8,128)} %fetch.1, bf16[16384,512]{1,0:T(8,128)(2,1)} %slab.1, bf16[1024,512]{1,0:T(8,128)(2,1)} %query.1, s32[8,128]{1,0:T(8,128)} %bitcast.8, s32[8,1,8]{2,1,0:T(1,128)} %lists.1, s32[8,1]{1,0:T(8,128)} %copy.12.counts, ...), custom_call_target="tpu_custom_call" | custom-call | flops 4294967296 | bytes 33554432 | tf_op jit(solution)/shard_map/tower/pallas_call | solution.py:263
  50.8 13.3 %score.1 = (f32[8,24,128]{2,1,0:T(8,128)}, bf16[16,64,512]{2,1,0:T(8,128)(2,1)}) custom-call(bf16[8,1024,512]{2,1,0:T(8,128)(2,1)} %get-tuple-element.7.queries, s32[8,16,128]{2,1,0:T(8,128)} %get-tuple-element.8.meta_all, bf16[16,64,512]{2,1,0:T(8,128)(2,1)} %get-tuple-element.9.cand_in, s32[16,512]{1,0:T(8,128)} %bitcast.6), custom_call_target="tpu_custom_call" | custom-call | flops 536870912 | bytes 10485760 | tf_op jit(solution)/shard_map/score/pallas_call | solution.py:386
  64.2 0.0 copy-start
  64.2 0.9 %copy-done = f32[8,24,128]{2,1,0:T(8,128)S(1)} copy-done((f32[8,24,128]{2,1,0:T(8,128)S(1)}, f32[8,24,128]{2,1,0:T(8,128)}, u32[]{:S(2)}) %copy-start) | copy-done | bytes 98328
  65.1 14.4 %merge.1 = f32[8,128]{1,0:T(8,128)S(1)} custom-call(f32[8,24,128]{2,1,0:T(8,128)S(1)} %copy-done), custom_call_target="tpu_custom_call" | custom-call | tf_op jit(solution)/shard_map/merge/pallas_call | solution.py:489
  79.5 0.6 copy.14
Async XLA Ops:
  64.2 0.9 %copy-start = (f32[8,24,128]{2,1,0:T(8,128)S(1)}, f32[8,24,128]{2,1,0:T(8,128)}, u32[]{:S(2)}) copy-start(f32[8,24,128]{2,1,0:T(8,128)} %get-tuple-element.11.stats) | copy-start | bytes 294916

commit v2 on v1

v2 whole, which is shorter than its diff:
```python
import functools

import jax
import jax.numpy as jnp
from jax import lax
from jax.experimental import pallas as pl
from jax.experimental.pallas import tpu as pltpu
from jax.sharding import PartitionSpec as P

MESH = pl.DeviceIdType.MESH
ANY = pl.BlockSpec(memory_space=pl.ANY)
VMEM = pl.BlockSpec(memory_space=pltpu.VMEM)
SMEM = pl.BlockSpec(memory_space=pltpu.SMEM)

E = 512
H = 2048
NC = 16
NX = 4
ND = 2
NJ = NX * ND
SUB = 64
LIST = 8
ROWS = 16384
QROWS = 1024
QB = QROWS // 128
HALF = QROWS // 2
SLAB_CHUNK = 512
OWNERS = 2
LOW = -1e30


def flip(value, bits, width):
    out = value
    for bit in range(width):
        if (bits >> bit) & 1:
            out = out + (1 << bit) * (1 - 2 * ((value // (1 << bit)) % 2))
    return out


FLOWS = (
    ("y", (0, 0), 0, 256, None),
    ("r", (0, 0), 0, 256, None),
    ("l", (0, 0), 256, 256, None),
    ("y", (0, 0), 256, 256, None),
    ("r", (0, 0), 256, 256, None),
    ("l", (0, 0), 0, 256, None),
    ("r", (-1, 0), 0, 256, 1),
    ("l", (1, 0), 256, 256, 2),
    ("r", (0, 1), 0, 256, 0),
    ("l", (0, 1), 0, 256, 0),
    ("y", (1, 0), 256, 256, 2),
    ("y", (-1, 0), 256, 256, 4),
    ("y", (2, 0), 256, 256, 7),
    ("r", (-1, 1), 0, 128, 8),
    ("l", (1, 1), 128, 128, 9),
)


def landed(flow):
    hop, (ox, oy), *_ = FLOWS[flow]
    ox, oy = {"r": (ox - 1, oy), "l": (ox + 1, oy), "y": (ox, 1 - oy)}[hop]
    return (2 if ox == -2 else ox), oy


def merged(parts):
    tops = [part[0] for part in parts]
    top = functools.reduce(jnp.maximum, tops)
    total = functools.reduce(jnp.add, [part[1] * jnp.exp(part[0] - top) for part in parts])
    positive = functools.reduce(jnp.add, [part[2] for part in parts])
    return top, total, positive


def thirds(ref, index):
    return tuple(ref[index, n * QB : (n + 1) * QB, :] for n in range(3))


def thirds(ref, index):
    return tuple(ref[index, n] for n in range(3))


def kernel(
    fetch, slab, query, pos, lists, counts, item_counts, w_in, b_in, w_out,
    cand_out, loss,
    chunk, table, rowbuf, staged, arrived, meta, meta_all, w_in_v, w_out_v, cand, queries, logt, neg_log, member, wanted,
    stats, by_group, part, by_catalog,
    slab_sem, w_sem, own_sem, meta_send, meta_recv, a2a_send, a2a_recv, flow_send, flow_recv, core_send, core_recv, out_sem,
    send_a, recv_a, send_b, recv_b,
):
    t = lax.axis_index("catalog")
    x = lax.axis_index("query")
    d = lax.axis_index("dp")
    core = t % 2
    j = x * ND + d

    own_query = pltpu.make_async_copy(query, queries.at[j], own_sem.at[0])
    n_chunks = ROWS // SLAB_CHUNK
    depth = chunk.shape[0]

    def slab_copy(n):
        slot = n % depth
        rows = pl.ds(pl.multiple_of(n * SLAB_CHUNK, SLAB_CHUNK), SLAB_CHUNK)
        return pltpu.make_async_copy(slab.at[rows], chunk.at[slot], slab_sem.at[slot])

    for n in range(depth):
        slab_copy(n).start()

    own_query.start()

    meta_peers = [(dx, dd) for dx in range(NX) for dd in range(ND) if (dx, dd) != (0, 0)]
    right, left = (x + 1) % NX, (x + NX - 1) % NX
    hop_to = {
        "r": {"catalog": t, "query": right, "dp": d},
        "l": {"catalog": t, "query": left, "dp": d},
        "y": {"catalog": flip(t, 8, 4), "query": x, "dp": 1 - d},
    }
    sibling = {"catalog": flip(t, 1, 4), "query": x, "dp": d}

    barrier = pltpu.get_barrier_semaphore()
    n_peers = 0
    for k in range(1, NC):
        pl.semaphore_signal(barrier, inc=1, device_id={"catalog": flip(t, k, 4), "query": x, "dp": d}, device_id_type=MESH)
        n_peers += 1
    for dx, dd in meta_peers:
        pl.semaphore_signal(
            barrier, inc=1, device_id={"catalog": t, "query": (x + dx) % NX, "dp": (d + dd) % ND}, device_id_type=MESH
        )
        n_peers += 1
    pl.semaphore_signal(barrier, inc=1, device_id=hop_to["y"], device_id_type=MESH)
    n_peers += 1

    square = (QB, LIST)
    diagonal = lax.broadcasted_iota(jnp.int32, square, 0) == lax.broadcasted_iota(jnp.int32, square, 1)
    count = jnp.sum(jnp.where(diagonal, jnp.broadcast_to(counts[...], square), 0), axis=1, keepdims=True)
    listed = jnp.where(lax.broadcasted_iota(jnp.int32, square, 1) < count, lists[:, 0, :], -1)
    meta[...] = jnp.full_like(meta, -1)
    meta[0:QB, :] = pos[...]
    meta[QB : 2 * QB, 0:LIST] = listed

    @pl.loop(0, n_chunks)
    def _(n):
        slot = n % depth
        slab_copy(n).wait()

        @pl.loop(0, SLAB_CHUNK // 64)
        def _(i):
            rows = pl.ds(pl.multiple_of(i * 64, 64), 64)
            to = pl.ds(pl.multiple_of(n * SLAB_CHUNK + i * 64, 64), 64)
            table[to, :] = chunk[slot, rows, :].astype(jnp.float32)

        @pl.when(n + depth < n_chunks)
        def _():
            slab_copy(n + depth).start()

    pl.semaphore_wait(barrier, n_peers)

    def origin(place):
        ox, oy = place
        xo = (x + ox + NX) % NX
        return xo * ND + (1 - d if oy else d)

    def flow_copy(n):
        hop, place, first, count, _ = FLOWS[n]
        jo = origin(place)
        rows = pl.ds(pl.multiple_of(core * HALF + first, 128), count)
        src = query.at[rows] if place == (0, 0) else queries.at[jo, rows]
        return pltpu.make_async_remote_copy(
            src_ref=src,
            dst_ref=queries.at[jo, rows],
            send_sem=flow_send.at[n],
            recv_sem=flow_recv.at[n],
            device_id=hop_to[hop],
            device_id_type=MESH,
        )

    def core_copy(n):
        _, _, first, count, _ = FLOWS[n]
        jo = origin(landed(n))
        rows = pl.ds(pl.multiple_of(core * HALF + first, 128), count)
        return pltpu.make_async_remote_copy(
            src_ref=queries.at[jo, rows],
            dst_ref=queries.at[jo, rows],
            send_sem=core_send.at[n],
            recv_sem=core_recv.at[n],
            device_id=sibling,
            device_id_type=MESH,
        )

    def advance(flows):
        for n in flows:
            flow_copy(n).wait_recv()
            for later, flow in enumerate(FLOWS):
                if flow[4] == n:
                    flow_copy(later).start()
            core_copy(n).start()

    for n, flow in enumerate(FLOWS):
        if flow[4] is None:
            flow_copy(n).start()

    def meta_copy(n):
        dx, dd = meta_peers[n]
        return pltpu.make_async_remote_copy(
            src_ref=meta,
            dst_ref=meta_all.at[j],
            send_sem=meta_send.at[n],
            recv_sem=meta_recv.at[n],
            device_id={"catalog": t, "query": (x + dx) % NX, "dp": (d + dd) % ND},
            device_id_type=MESH,
        )

    for n in range(len(meta_peers)):
        meta_copy(n).start()
    w_in_copy = pltpu.make_async_copy(w_in, w_in_v, w_sem.at[0])
    w_out_copy = pltpu.make_async_copy(w_out, w_out_v, w_sem.at[1])
    w_in_copy.start()
    w_out_copy.start()

    def a2a_copy(k):
        to = flip(t, k, 4)
        return pltpu.make_async_remote_copy(
            src_ref=staged.at[k],
            dst_ref=arrived.at[t],
            send_sem=a2a_send.at[k],
            recv_sem=a2a_recv.at[k],
            device_id={"catalog": to, "query": x, "dp": d},
            device_id_type=MESH,
        )

    for k in range(NC - 1, -1, -1):
        to = flip(t, k, 4)

        @pl.loop(0, SUB // 16)
        def _(i):
            for u in range(16):
                row = fetch[0, to, i * 16 + u]
                rowbuf[pl.ds(i * 16 + u, 1), :] = table[pl.ds(row, 1), :]

        if k:
            staged[k] = rowbuf[...].astype(jnp.bfloat16)
            a2a_copy(k).start()
        else:
            arrived[t] = rowbuf[...].astype(jnp.bfloat16)

    advance((0, 1, 2))
    w_in_copy.wait()
    w_out_copy.wait()

    def tower(group):
        base = 4 * flip(t // 4, group, 2)
        for k in range(4 * group, 4 * group + 4):
            if k:
                a2a_copy(k).wait_recv()
        rows = arrived[pl.ds(base, 4)].reshape(4 * SUB, E)
        hidden = jnp.maximum(jnp.dot(rows, w_in_v[...], preferred_element_type=jnp.float32) + b_in[...], 0.0).astype(jnp.bfloat16)
        y = jnp.dot(hidden, w_out_v[...], preferred_element_type=jnp.float32)
        normed = y * lax.rsqrt(jnp.sum(y * y, axis=-1, keepdims=True) + 1e-06)
        cand[pl.ds(base, 4)] = normed.astype(jnp.bfloat16).reshape(4, SUB, E)
        pltpu.make_async_copy(cand.at[pl.ds(base, 4)], cand_out.at[pl.ds(base, 4)], out_sem.at[group]).start()

    logt[...] = jnp.transpose(-jnp.log(item_counts[...].astype(jnp.float32)))
    own = logt[pl.ds(pl.multiple_of(j * SUB, SUB), SUB), :]
    for o in range(NC):
        neg_log[o * SUB : (o + 1) * SUB, :] = jnp.broadcast_to(own[:, o : o + 1], (SUB, 128))

    for n in range(len(meta_peers)):
        meta_copy(n).wait_recv()
    meta_all[j] = meta[...]
    owner_block = lax.broadcasted_iota(jnp.int32, (NC, 128), 0) * 4 + x

    @pl.loop(0, NJ)
    def _(jo):
        offset = meta_all[jo, 0:QB, :] - (t * (NC * 512) + j * SUB)
        here = (offset >= 0) & (offset < NC * 512) & ((offset & 511) < SUB)
        wanted[jo] = jnp.where(here, (offset >> 9) * SUB + (offset & 511), -1)
        for b in range(QB):
            row = meta_all[jo, QB + b : QB + b + 1, :]
            hit = jnp.zeros((NC, 128), jnp.int32)
            for e in range(LIST):
                hit = hit | (jnp.broadcast_to(row[:, e : e + 1], (NC, 128)) == owner_block).astype(jnp.int32)
            member[jo, b] = hit

    tower(0)
    advance((3, 4, 5))
    tower(1)
    advance((7, 6, 8, 9))
    tower(2)
    tower(3)

    row_ids = lax.broadcasted_iota(jnp.int32, (8, 128), 0)
    wide = OWNERS * SUB

    def score(place):
        jo = origin(place)

        @pl.loop(0, QB // 2)
        def _(pair):
            rows = queries[jo, pl.ds(pl.multiple_of(pair * 256, 256), 256), :]
            low = jnp.full((8, 128), LOW, jnp.float32)
            top, total, positive = [low, low], [jnp.zeros_like(low)] * 2, [jnp.zeros_like(low)] * 2
            want = [jnp.broadcast_to(wanted[jo, pl.ds(pair * 2 + h, 1), :], (8, 128)) for h in range(2)]
            for step in range(NC // OWNERS):
                scores = lax.dot_general(
                    cand[step * OWNERS : (step + 1) * OWNERS].reshape(wide, E),
                    rows,
                    (((1,), (1,)), ((), ())),
                    preferred_element_type=jnp.float32,
                )
                for h in range(2):
                    tiles, peak = [], low
                    for o in range(OWNERS):
                        owner = step * OWNERS + o
                        mine = []
                        for i in range(SUB // 8):
                            at = o * SUB + i * 8
                            tile = scores[at : at + 8, h * 128 : (h + 1) * 128]
                            tile = tile + neg_log[step * wide + at : step * wide + at + 8, :]
                            positive[h] = jnp.where(row_ids == want[h] - (step * wide + at), tile, positive[h])
                            mine.append(tile)
                        hit = jnp.broadcast_to(member[jo, pair * 2 + h, owner : owner + 1, :], (8, 128)) > 0
                        peak = jnp.maximum(peak, jnp.where(hit, functools.reduce(jnp.maximum, mine), LOW))
                        tiles.append((hit, mine))
                    mass = jnp.zeros_like(low)
                    for hit, mine in tiles:
                        mass = mass + jnp.where(hit, functools.reduce(jnp.add, [jnp.exp(tile - peak) for tile in mine]), 0.0)
                    new = jnp.maximum(top[h], peak)
                    total[h] = total[h] * jnp.exp(top[h] - new) + mass * jnp.exp(peak - new)
                    top[h] = new
            for h in range(2):
                peak = jnp.max(top[h], axis=0, keepdims=True)
                at = pl.ds(pair * 2 + h, 1)
                stats[jo, 0, at, :] = peak
                stats[jo, 1, at, :] = jnp.sum(total[h] * jnp.exp(top[h] - peak), axis=0, keepdims=True)
                stats[jo, 2, at, :] = jnp.sum(positive[h], axis=0, keepdims=True)

    def group_copy(place):
        ox, oy = place
        n = meta_peers.index(((ox + NX) % NX, oy))
        jo = origin(place)
        return pltpu.make_async_remote_copy(
            src_ref=stats.at[jo],
            dst_ref=by_group.at[j],
            send_sem=send_a.at[n],
            recv_sem=recv_a.at[n],
            device_id={"catalog": t, "query": (x + ox + NX) % NX, "dp": 1 - d if oy else d},
            device_id_type=MESH,
        )

    def finish(place):
        for n in range(len(FLOWS)):
            if landed(n) == place:
                core_copy(n).wait_recv()
        score(place)
        group_copy(place).start()

    own_query.wait()
    score((0, 0))
    finish((0, 1))
    finish((1, 0))
    advance((10, 11, 12))
    finish((-1, 0))
    advance((13, 14))
    finish((2, 0))
    finish((1, 1))
    finish((-1, 1))
    finish((2, 1))

    by_group[j] = stats[j]
    places = [(0, 1), (1, 0), (-1, 0), (2, 0), (1, 1), (-1, 1), (2, 1)]
    for place in places:
        group_copy(place).wait_recv()
    for n, value in enumerate(merged([thirds(by_group, i) for i in range(NJ)])):
        part[n] = value

    def catalog_copy(k):
        return pltpu.make_async_remote_copy(
            src_ref=part,
            dst_ref=by_catalog.at[t],
            send_sem=send_b.at[k],
            recv_sem=recv_b.at[k],
            device_id={"catalog": flip(t, k, 4), "query": x, "dp": d},
            device_id_type=MESH,
        )

    for k in range(NC - 1, 0, -1):
        catalog_copy(k).start()
    by_catalog[t] = part[...]

    for group in range(4):
        base = 4 * flip(t // 4, group, 2)
        pltpu.make_async_copy(cand.at[pl.ds(base, 4)], cand_out.at[pl.ds(base, 4)], out_sem.at[group]).wait()
    for k in range(1, NC):
        a2a_copy(k).wait_send()
    for n in range(len(FLOWS)):
        flow_copy(n).wait_send()
        core_copy(n).wait_send()
    for n in range(len(meta_peers)):
        meta_copy(n).wait_send()
    for place in places:
        group_copy(place).wait_send()

    for k in range(NC - 1, 0, -1):
        catalog_copy(k).wait_recv()
    top, total, positive = merged([thirds(by_catalog, i) for i in range(NC)])
    loss[...] = top + jnp.log(total) - positive
    for k in range(1, NC):
        catalog_copy(k).wait_send()


def per_device(
    slab, fetch_rows, w_in, b_in, w_out, query_emb, item_counts, tile_blocks, tile_count, pos_idx
):
    dma = pltpu.SemaphoreType.DMA
    bf16, f32, i32 = jnp.bfloat16, jnp.float32, jnp.int32
    cand, loss = pl.pallas_call(
        kernel,
        out_shape=(
            jax.ShapeDtypeStruct((NC, SUB, E), bf16),
            jax.ShapeDtypeStruct((QB, 128), f32),
        ),
        in_specs=[SMEM, ANY, ANY, VMEM, VMEM, VMEM, VMEM, ANY, VMEM, ANY],
        out_specs=(ANY, VMEM),
        scratch_shapes=[
            pltpu.VMEM((4, SLAB_CHUNK, E), bf16),
            pltpu.VMEM((ROWS, E), f32),
            pltpu.VMEM((SUB, E), f32),
            pltpu.VMEM((NC, SUB, E), bf16),
            pltpu.VMEM((NC, SUB, E), bf16),
            pltpu.VMEM((2 * QB, 128), i32),
            pltpu.VMEM((NJ, 2 * QB, 128), i32),
            pltpu.VMEM((E, H), bf16),
            pltpu.VMEM((H, E), bf16),
            pltpu.VMEM((NC, SUB, E), bf16),
            pltpu.VMEM((NJ, QROWS, E), bf16),
            pltpu.VMEM((512, NC), f32),
            pltpu.VMEM((NC * SUB, 128), f32),
            pltpu.VMEM((NJ, QB, NC, 128), i32),
            pltpu.VMEM((NJ, QB, 128), i32),
            pltpu.VMEM((NJ, 3, QB, 128), f32),
            pltpu.VMEM((NJ, 3, QB, 128), f32),
            pltpu.VMEM((3, QB, 128), f32),
            pltpu.VMEM((NC, 3, QB, 128), f32),
            dma((4,)),
            dma((2,)),
            dma((1,)),
            dma((NJ - 1,)),
            dma((NJ - 1,)),
            dma((NC,)),
            dma((NC,)),
            dma((len(FLOWS),)),
            dma((len(FLOWS),)),
            dma((len(FLOWS),)),
            dma((len(FLOWS),)),
            dma((4,)),
            dma((NJ - 1,)),
            dma((NJ - 1,)),
            dma((NC,)),
            dma((NC,)),
        ],
        compiler_params=pltpu.CompilerParams(
            collective_id=0, has_side_effects=True, vmem_limit_bytes=60 * 1024 * 1024
        ),
        cost_estimate=pl.CostEstimate(flops=12 << 30, bytes_accessed=32 << 20, transcendentals=1 << 23),
        name="two_tower",
    )(
        fetch_rows,
        slab,
        query_emb,
        pos_idx.reshape(QB, 128),
        tile_blocks,
        tile_count.reshape(1, QB),
        item_counts.reshape(NC, 512),
        w_in,
        b_in.reshape(1, H),
        w_out,
    )
    return (cand[None], loss.reshape(QROWS))


def solution(mesh):
    in_specs = (
        P("catalog", None),
        P("catalog", None, ("query", "dp")),
        P(),
        P(),
        P(),
        P(("query", "dp"), None),
        P("catalog", None, None),
        P(("query", "dp"), "catalog", None),
        P(("query", "dp"), "catalog"),
        P(("query", "dp")),
    )
    out_specs = (P("catalog", None, ("query", "dp"), None), P(("query", "dp")))
    return jax.shard_map(
        per_device, mesh=mesh, in_specs=in_specs, out_specs=out_specs, check_vma=False
    )
```

time: 80.4 us -> 89.4 us (1.11)
  Pallas kernels: 76.6 us -> 85.5 us
    pallas_call x3 -> x1, Pallas kernels: 76.6 us -> 85.5 us  [per_device(): pl.pallas_call(kernel, out_shape=(jax.ShapeDtypeStruct((NC, SUB, E), bf16...]
where the time goes in v2:
time: 89.4 us; the launch traced here: 89 us
  Pallas kernels  85.5 us (96%)
  local copies, waits for them, and re-layouts  2.89 us (3%)
    pallas_call x1, Pallas kernels, per_device(): pl.pallas_call(kernel, out_shape=(jax.ShapeDtypeStruct((NC, SUB, E), bf16...  85.5 us
    unnamed x4, local copies, waits for them, and re-layouts  2.89 us

profile of v2, /device:TPU:1, one launch (start us, length us, event | category | flops | bytes accessed | tf_op | source)
XLA Modules:
  0.0 89.0 jit_solution(10318933587880995402)
XLA Ops:
  0.6 85.5 %two_tower.1 = (bf16[16,64,512]{2,1,0:T(8,128)(2,1)}, f32[8,128]{1,0:T(8,128)}) custom-call(s32[1,16,64]{2,1,0:T(8,128)} %fetch.1, bf16[16384,512]{1,0:T(8,128)(2,1)} %slab.1, bf16[1024,512]{1,0:T(8,128)(2,1)} %query.1, s32[8,128]{1,0:T(8,128)} %bitcast.10, s32[8,1,8]{2,1,0:T(1,128)} %lists.1, s32[1,8]{1,0:T(1,128)} %bitcast.11, s32[16,512]{1,0:T(8,128)} %bitcast.8, ...), custom_call_target="tpu_custom_call" | custom-call | flops 12884901888 | bytes 33554432 | tf_op jit(solution)/shard_map/two_tower/pallas_call | solution.py:414
  86.1 0.0 copy-start
  86.1 2.3 %copy.14 = bf16[1,16,64,512]{3,2,1,0:T(8,128)(2,1)} copy(bf16[1,16,64,512]{3,2,1,0:T(8,128)(2,1)} %bitcast.6) | data formatting | bytes 2097152
  88.4 0.0 copy-done
  88.4 0.6 copy.15
Async XLA Ops:
  86.1 2.3 %copy-start = (f32[8,128]{1,0:T(8,128)S(1)}, f32[8,128]{1,0:T(8,128)}, u32[]{:S(2)}) copy-start(f32[8,128]{1,0:T(8,128)} %get-tuple-element.5) | copy-start | bytes 12292

commit v3 on v1

v3 whole, which is shorter than its diff:
```python
import functools

import jax
import jax.numpy as jnp
from jax import lax
from jax.experimental import pallas as pl
from jax.experimental.pallas import tpu as pltpu
from jax.sharding import PartitionSpec as P

MESH = pl.DeviceIdType.MESH
ANY = pl.BlockSpec(memory_space=pl.ANY)
VMEM = pl.BlockSpec(memory_space=pltpu.VMEM)
SMEM = pl.BlockSpec(memory_space=pltpu.SMEM)

E = 512
H = 2048
NC = 16
NX = 4
ND = 2
NJ = NX * ND
SUB = 64
LIST = 8
ROWS = 16384
QROWS = 1024
QB = QROWS // 128
HALF = QROWS // 2
SLAB_CHUNK = 1024
JOBS = 4
NONE = 256
LOW = -1e30
VMEM_LIMIT = 60 * 1024 * 1024


def flip(value, bits, width):
    out = value
    for bit in range(width):
        if (bits >> bit) & 1:
            out = out + (1 << bit) * (1 - 2 * ((value // (1 << bit)) % 2))
    return out


FLOWS = {}
for _n in (0, 128):
    FLOWS |= {
        f"y{_n}": ("y", (0, 0), _n, 128, None),
        f"r{_n}": ("r", (0, 0), _n, 128, None),
        f"l{_n + 256}": ("l", (0, 0), _n + 256, 128, None),
    }
for _n in (0, 128):
    FLOWS |= {
        f"y{_n + 256}": ("y", (0, 0), _n + 256, 128, None),
        f"r{_n + 256}": ("r", (0, 0), _n + 256, 128, None),
        f"l{_n}": ("l", (0, 0), _n, 128, None),
    }
for _n in (0, 128):
    FLOWS |= {
        f"rr{_n}": ("r", (-1, 0), _n, 128, f"r{_n}"),
        f"ll{_n + 256}": ("l", (1, 0), _n + 256, 128, f"l{_n + 256}"),
        f"yr{_n}": ("r", (0, 1), _n, 128, f"y{_n}"),
        f"yl{_n}": ("l", (0, 1), _n, 128, f"y{_n}"),
        f"ly{_n}": ("y", (1, 0), _n + 256, 128, f"l{_n + 256}"),
        f"ry{_n}": ("y", (-1, 0), _n + 256, 128, f"r{_n + 256}"),
        f"lly{_n}": ("y", (2, 0), _n + 256, 128, f"ll{_n + 256}"),
    }
FLOWS |= {
    "yrr": ("r", (-1, 1), 0, 128, "yr0"),
    "yll": ("l", (1, 1), 128, 128, "yl128"),
}
NAMES = tuple(FLOWS)
PLACES = ((0, 0), (0, 1), (1, 0), (-1, 0), (2, 0), (1, 1), (-1, 1), (2, 1))


def landed(name):
    hop, (ox, oy), *_ = FLOWS[name]
    ox, oy = {"r": (ox - 1, oy), "l": (ox + 1, oy), "y": (ox, 1 - oy)}.get(hop, (ox, oy))
    return (2 if ox == -2 else ox), oy


def tower_kernel(
    fetch, slab, query, pos, lists, counts, item_counts, w_in, b_in, w_out,
    queries_out, meta_all, wanted, neg_log, cand,
    queries, chunk, table, rowbuf, staged, arrived, meta, w_in_v, w_out_v, logt,
    slab_sem, w_sem, own_sem, meta_send, meta_recv, a2a_send, a2a_recv, flow_send, flow_recv, core_send, core_recv, out_sem,
):
    t = lax.axis_index("catalog")
    x = lax.axis_index("query")
    d = lax.axis_index("dp")
    core = t % 2
    j = x * ND + d

    own_query = pltpu.make_async_copy(query, queries.at[j], own_sem.at[0])
    n_chunks = ROWS // SLAB_CHUNK
    depth = chunk.shape[0]

    def slab_copy(n):
        slot = n % depth
        rows = pl.ds(pl.multiple_of(n * SLAB_CHUNK, SLAB_CHUNK), SLAB_CHUNK)
        return pltpu.make_async_copy(slab.at[rows], chunk.at[slot], slab_sem.at[slot])

    for n in range(depth):
        slab_copy(n).start()

    own_query.start()

    meta_peers = [(dx, dd) for dx in range(NX) for dd in range(ND) if (dx, dd) != (0, 0)]
    right, left = (x + 1) % NX, (x + NX - 1) % NX
    hop_to = {
        "r": {"catalog": t, "query": right, "dp": d},
        "l": {"catalog": t, "query": left, "dp": d},
        "y": {"catalog": flip(t, 8, 4), "query": x, "dp": 1 - d},
    }
    sibling = {"catalog": flip(t, 1, 4), "query": x, "dp": d}

    barrier = pltpu.get_barrier_semaphore()
    n_peers = 0
    for k in range(1, NC):
        pl.semaphore_signal(barrier, inc=1, device_id={"catalog": flip(t, k, 4), "query": x, "dp": d}, device_id_type=MESH)
        n_peers += 1
    for dx, dd in meta_peers:
        pl.semaphore_signal(
            barrier, inc=1, device_id={"catalog": t, "query": (x + dx) % NX, "dp": (d + dd) % ND}, device_id_type=MESH
        )
        n_peers += 1
    pl.semaphore_signal(barrier, inc=1, device_id=hop_to["y"], device_id_type=MESH)
    n_peers += 1

    square = (QB, LIST)
    diagonal = lax.broadcasted_iota(jnp.int32, square, 0) == lax.broadcasted_iota(jnp.int32, square, 1)
    count = jnp.sum(jnp.where(diagonal, jnp.broadcast_to(counts[...], square), 0), axis=1, keepdims=True)
    listed = jnp.where(lax.broadcasted_iota(jnp.int32, square, 1) < count, lists[:, 0, :], NONE)
    meta[...] = jnp.full_like(meta, NONE)
    meta[0:QB, :] = pos[...]
    meta[QB : 2 * QB, 0:LIST] = listed

    pl.semaphore_wait(barrier, n_peers)

    def origin(place):
        ox, oy = place
        xo = (x + ox + NX) % NX
        return xo * ND + (1 - d if oy else d)

    def flow_copy(name):
        hop, place, first, count, _ = FLOWS[name]
        jo = origin(place)
        rows = pl.ds(pl.multiple_of(core * HALF + first, 128), count)
        src = query.at[rows] if place == (0, 0) else queries.at[jo, rows]
        return pltpu.make_async_remote_copy(
            src_ref=src,
            dst_ref=queries.at[jo, rows],
            send_sem=flow_send.at[NAMES.index(name)],
            recv_sem=flow_recv.at[NAMES.index(name)],
            device_id=hop_to[hop],
            device_id_type=MESH,
        )

    def core_copy(name):
        _, _, first, count, _ = FLOWS[name]
        part = queries.at[origin(landed(name)), pl.ds(pl.multiple_of(core * HALF + first, 128), count)]
        return pltpu.make_async_remote_copy(
            src_ref=part,
            dst_ref=part,
            send_sem=core_send.at[NAMES.index(name)],
            recv_sem=core_recv.at[NAMES.index(name)],
            device_id=sibling,
            device_id_type=MESH,
        )

    received, sent = set(), set()

    def send_ready():
        for name, flow in FLOWS.items():
            if name not in sent and (flow[4] is None or flow[4] in received):
                sent.add(name)
                flow_copy(name).start()

    def advance(*names):
        for name in names:
            flow_copy(name).wait_recv()
            received.add(name)
            send_ready()
            core_copy(name).start()

    send_ready()

    def meta_copy(n):
        dx, dd = meta_peers[n]
        return pltpu.make_async_remote_copy(
            src_ref=meta,
            dst_ref=meta_all.at[j],
            send_sem=meta_send.at[n],
            recv_sem=meta_recv.at[n],
            device_id={"catalog": t, "query": (x + dx) % NX, "dp": (d + dd) % ND},
            device_id_type=MESH,
        )

    for n in range(len(meta_peers)):
        meta_copy(n).start()
    def widen(first, count):
        @pl.loop(first, first + count)
        def _(n):
            slot = n % depth
            slab_copy(n).wait()

            @pl.loop(0, SLAB_CHUNK // 64)
            def _(i):
                rows = pl.ds(pl.multiple_of(i * 64, 64), 64)
                to = pl.ds(pl.multiple_of(n * SLAB_CHUNK + i * 64, 64), 64)
                table[to, :] = chunk[slot, rows, :].astype(jnp.float32)

            @pl.when(n + depth < n_chunks)
            def _():
                slab_copy(n + depth).start()

    widen(0, n_chunks // 2)
    advance("y0", "r0", "l256")
    widen(n_chunks // 2, n_chunks // 2)
    w_in_copy = pltpu.make_async_copy(w_in, w_in_v, w_sem.at[0])
    w_out_copy = pltpu.make_async_copy(w_out, w_out_v, w_sem.at[1])
    w_in_copy.start()
    w_out_copy.start()

    def a2a_copy(k):
        to = flip(t, k, 4)
        return pltpu.make_async_remote_copy(
            src_ref=staged.at[k],
            dst_ref=arrived.at[t],
            send_sem=a2a_send.at[k],
            recv_sem=a2a_recv.at[k],
            device_id={"catalog": to, "query": x, "dp": d},
            device_id_type=MESH,
        )

    for k in range(NC - 1, -1, -1):
        to = flip(t, k, 4)

        @pl.loop(0, SUB // 16)
        def _(i):
            for u in range(16):
                row = fetch[0, to, i * 16 + u]
                rowbuf[pl.ds(i * 16 + u, 1), :] = table[pl.ds(row, 1), :]

        if k:
            staged[k] = rowbuf[...].astype(jnp.bfloat16)
        else:
            arrived[t] = rowbuf[...].astype(jnp.bfloat16)
        if k == 12:
            advance("y128", "r128", "l384")
        if k == 6:
            advance("r256", "l0", "y256")
        if k:
            a2a_copy(k).start()

    advance("rr0", "ll256", "yr0", "yl0", "r384", "l128", "y384")
    w_in_copy.wait()
    w_out_copy.wait()

    def tower(group):
        base = 4 * flip(t // 4, group, 2)
        for k in range(4 * group, 4 * group + 4):
            if k:
                a2a_copy(k).wait_recv()
        rows = arrived[pl.ds(base, 4)].reshape(4 * SUB, E)
        hidden = jnp.maximum(jnp.dot(rows, w_in_v[...], preferred_element_type=jnp.float32) + b_in[...], 0.0).astype(jnp.bfloat16)
        y = jnp.dot(hidden, w_out_v[...], preferred_element_type=jnp.float32)
        normed = y * lax.rsqrt(jnp.sum(y * y, axis=-1, keepdims=True) + 1e-06)
        cand[pl.ds(base, 4)] = normed.astype(jnp.bfloat16).reshape(4, SUB, E)

    logt[...] = jnp.transpose(-jnp.log(item_counts[...].astype(jnp.float32)))
    own = logt[pl.ds(pl.multiple_of(j * SUB, SUB), SUB), :]
    for o in range(NC):
        neg_log[o * SUB : (o + 1) * SUB, :] = jnp.broadcast_to(own[:, o : o + 1], (SUB, 128))

    for n in range(len(meta_peers)):
        meta_copy(n).wait_recv()
    meta_all[j] = meta[...]
    for jo in range(NJ):
        offset = meta_all[jo, 0:QB, :] - (t * (NC * 512) + j * SUB)
        here = (offset >= 0) & (offset < NC * 512) & ((offset & 511) < SUB)
        wanted[jo] = jnp.where(here, (offset >> 9) * SUB + (offset & 511), -1)

    def query_out(place):
        jo = origin(place)
        return pltpu.make_async_copy(queries.at[jo], queries_out.at[jo], out_sem.at[PLACES.index(place)])

    def ship(*places):
        for place in places:
            for name in NAMES:
                if landed(name) == place:
                    core_copy(name).wait_recv()
            query_out(place).start()

    own_query.wait()
    query_out((0, 0)).start()
    advance("ly0", "ry0", "rr128", "ll384")
    tower(0)
    ship((0, 1), (1, 0), (-1, 0))
    advance("yr128", "yl128")
    tower(1)
    ship((2, 0))
    advance("ly128", "ry128", "lly0")
    tower(2)
    ship((1, 1), (-1, 1))
    tower(3)
    advance("yrr", "yll", "lly128")
    ship((2, 1))
    assert len(received) == len(sent) == len(NAMES)

    for place in PLACES:
        query_out(place).wait()
    for k in range(1, NC):
        a2a_copy(k).wait_send()
    for name in NAMES:
        flow_copy(name).wait_send()
        core_copy(name).wait_send()
    for n in range(len(meta_peers)):
        meta_copy(n).wait_send()


def run_tower(fetch, slab, query, pos, lists, counts, item_counts, w_in, b_in, w_out):
    dma = pltpu.SemaphoreType.DMA
    bf16, f32, i32 = jnp.bfloat16, jnp.float32, jnp.int32
    return pl.pallas_call(
        tower_kernel,
        out_shape=(
            jax.ShapeDtypeStruct((NJ, QROWS, E), bf16),
            jax.ShapeDtypeStruct((NJ, 2 * QB, 128), i32),
            jax.ShapeDtypeStruct((NJ, QB, 128), i32),
            jax.ShapeDtypeStruct((NC * SUB, 128), f32),
            jax.ShapeDtypeStruct((NC, SUB, E), bf16),
        ),
        in_specs=[SMEM, ANY, ANY, VMEM, VMEM, VMEM, VMEM, ANY, VMEM, ANY],
        out_specs=(ANY, VMEM, VMEM, VMEM, VMEM),
        scratch_shapes=[
            pltpu.VMEM((NJ, QROWS, E), bf16),
            pltpu.VMEM((8, SLAB_CHUNK, E), bf16),
            pltpu.VMEM((ROWS, E), f32),
            pltpu.VMEM((SUB, E), f32),
            pltpu.VMEM((NC, SUB, E), bf16),
            pltpu.VMEM((NC, SUB, E), bf16),
            pltpu.VMEM((2 * QB, 128), i32),
            pltpu.VMEM((E, H), bf16),
            pltpu.VMEM((H, E), bf16),
            pltpu.VMEM((512, NC), f32),
            dma((8,)),
            dma((2,)),
            dma((1,)),
            dma((NJ - 1,)),
            dma((NJ - 1,)),
            dma((NC,)),
            dma((NC,)),
            dma((len(NAMES),)),
            dma((len(NAMES),)),
            dma((len(NAMES),)),
            dma((len(NAMES),)),
            dma((NJ,)),
        ],
        compiler_params=pltpu.CompilerParams(
            collective_id=0, has_side_effects=True, vmem_limit_bytes=VMEM_LIMIT
        ),
        cost_estimate=pl.CostEstimate(flops=4 * 1024 * E * H, bytes_accessed=32 << 20, transcendentals=0),
        name="tower",
    )(fetch, slab, query, pos, lists, counts, item_counts, w_in, b_in, w_out)


def score_kernel(
    queries, meta, wanted, neg_log, cand,
    stats, cand_out,
    q, jobs, top, total, positive, q_sem, sem,
):
    x = lax.axis_index("query")
    cand_store = pltpu.make_async_copy(cand, cand_out, sem.at[0])
    loads = [pltpu.make_async_copy(queries.at[n], q.at[n], q_sem.at[n]) for n in range(NJ)]
    for load in loads:
        load.start()
    cand_store.start()

    top[...] = jnp.full_like(top, LOW)
    total[...] = jnp.zeros_like(total)
    positive[...] = jnp.zeros_like(positive)

    def list_blocks(jo, n):
        for b in range(QB):
            for e in range(LIST):
                block = meta[jo, QB + b, e]
                jobs[n] = (jo * QB + b) * NC + (block >> 2)
                n = n + jnp.where((block & (NONE + 3)) == x, 1, 0)
        return n

    n_jobs = lax.fori_loop(0, NJ, list_blocks, jnp.int32(0))
    for u in range(JOBS):
        jobs[n_jobs + u] = NJ * QB * NC

    for load in loads:
        load.wait()
    row_ids = lax.broadcasted_iota(jnp.int32, (SUB, 128), 0)

    @pl.loop(0, (n_jobs + JOBS - 1) // JOBS)
    def _(step):
        found = []
        for u in range(JOBS):
            job = jobs[step * JOBS + u]
            b, o = job >> 4, job & (NC - 1)
            b_q = jnp.minimum(b, NJ * QB - 1)
            jo, b_j = b_q >> 3, b_q & (QB - 1)
            block = q[jo, pl.ds(pl.multiple_of(b_j * 128, 128), 128), :]
            scores = lax.dot_general(cand[o], block, (((1,), (1,)), ((), ())), preferred_element_type=jnp.float32)
            scores = scores + neg_log[pl.ds(pl.multiple_of(o * SUB, SUB), SUB), :]
            want = wanted[jo, pl.ds(b_j, 1), :] - o * SUB
            peak = jnp.max(scores, axis=0, keepdims=True)
            mass = jnp.sum(jnp.exp(scores - peak), axis=0, keepdims=True)
            match = jnp.sum(jnp.where(row_ids == want, scores, 0.0), axis=0, keepdims=True)
            found.append((b, peak, mass, match))
        for b, peak, mass, match in found:
            at = pl.ds(b, 1)
            old = top[at, :]
            new = jnp.maximum(old, peak)
            total[at, :] = total[at, :] * jnp.exp(old - new) + mass * jnp.exp(peak - new)
            positive[at, :] = positive[at, :] + match
            top[at, :] = new

    for n in range(NJ):
        stats[n, 0:QB, :] = top[n * QB : (n + 1) * QB, :]
        stats[n, QB : 2 * QB, :] = total[n * QB : (n + 1) * QB, :]
        stats[n, 2 * QB : 3 * QB, :] = positive[n * QB : (n + 1) * QB, :]
    cand_store.wait()


def run_score(queries, meta, wanted, neg_log, cand):
    return pl.pallas_call(
        score_kernel,
        out_shape=(
            jax.ShapeDtypeStruct((NJ, 3 * QB, 128), jnp.float32),
            jax.ShapeDtypeStruct((NC, SUB, E), jnp.bfloat16),
        ),
        in_specs=[ANY, SMEM, VMEM, VMEM, VMEM],
        out_specs=(VMEM, ANY),
        scratch_shapes=[
            pltpu.VMEM((NJ, QROWS, E), jnp.bfloat16),
            pltpu.SMEM((NJ * QB * LIST + 2 * JOBS,), jnp.int32),
            pltpu.VMEM((NJ * QB + 8, 128), jnp.float32),
            pltpu.VMEM((NJ * QB + 8, 128), jnp.float32),
            pltpu.VMEM((NJ * QB + 8, 128), jnp.float32),
            pltpu.SemaphoreType.DMA((NJ,)),
            pltpu.SemaphoreType.DMA((1,)),
        ],
        compiler_params=pltpu.CompilerParams(vmem_limit_bytes=VMEM_LIMIT),
        cost_estimate=pl.CostEstimate(flops=1 << 29, bytes_accessed=10 << 20, transcendentals=1 << 20),
        name="score",
    )(queries, meta, wanted, neg_log, cand)


def merged(parts):
    tops = [part[0] for part in parts]
    top = functools.reduce(jnp.maximum, tops)
    total = functools.reduce(jnp.add, [part[1] * jnp.exp(part[0] - top) for part in parts])
    positive = functools.reduce(jnp.add, [part[2] for part in parts])
    return top, total, positive


def thirds(ref, index):
    return tuple(ref[index, n * QB : (n + 1) * QB, :] for n in range(3))


def merge_kernel(stats, loss, by_group, part, by_catalog, send_a, recv_a, send_b, recv_b):
    t = lax.axis_index("catalog")
    x = lax.axis_index("query")
    d = lax.axis_index("dp")
    j = x * ND + d
    peers = [(dx, dd) for dx in range(NX) for dd in range(ND) if (dx, dd) != (0, 0)]

    def group_peer(n):
        dx, dd = peers[n]
        return (x + dx) % NX, (d + dd) % ND

    barrier = pltpu.get_barrier_semaphore()
    for n in range(NJ - 1):
        xp, dp = group_peer(n)
        pl.semaphore_signal(barrier, inc=1, device_id={"catalog": t, "query": xp, "dp": dp}, device_id_type=MESH)
    for k in range(1, NC):
        pl.semaphore_signal(barrier, inc=1, device_id={"catalog": flip(t, k, 4), "query": x, "dp": d}, device_id_type=MESH)
    pl.semaphore_wait(barrier, NJ - 1 + NC - 1)

    def group_copy(n):
        xp, dp = group_peer(n)
        return pltpu.make_async_remote_copy(
            src_ref=stats.at[xp * ND + dp],
            dst_ref=by_group.at[j],
            send_sem=send_a.at[n],
            recv_sem=recv_a.at[n],
            device_id={"catalog": t, "query": xp, "dp": dp},
            device_id_type=MESH,
        )

    for n in range(NJ - 1):
        group_copy(n).start()
    by_group[j] = stats[j]
    for n in range(NJ - 1):
        group_copy(n).wait_recv()
    for n, value in enumerate(merged([thirds(by_group, i) for i in range(NJ)])):
        part[n * QB : (n + 1) * QB, :] = value

    def catalog_copy(k):
        return pltpu.make_async_remote_copy(
            src_ref=part,
            dst_ref=by_catalog.at[t],
            send_sem=send_b.at[k],
            recv_sem=recv_b.at[k],
            device_id={"catalog": flip(t, k, 4), "query": x, "dp": d},
            device_id_type=MESH,
        )

    for k in range(NC - 1, 0, -1):
        catalog_copy(k).start()
    by_catalog[t] = part[...]
    for k in range(NC - 1, 0, -1):
        catalog_copy(k).wait_recv()
    top, total, positive = merged([thirds(by_catalog, i) for i in range(NC)])
    loss[...] = top + jnp.log(total) - positive
    for n in range(NJ - 1):
        group_copy(n).wait_send()
    for k in range(1, NC):
        catalog_copy(k).wait_send()


def run_merge(stats):
    dma = pltpu.SemaphoreType.DMA
    return pl.pallas_call(
        merge_kernel,
        out_shape=jax.ShapeDtypeStruct((QB, 128), jnp.float32),
        in_specs=[VMEM],
        out_specs=VMEM,
        scratch_shapes=[
            pltpu.VMEM((NJ, 3 * QB, 128), jnp.float32),
            pltpu.VMEM((3 * QB, 128), jnp.float32),
            pltpu.VMEM((NC, 3 * QB, 128), jnp.float32),
            dma((NJ - 1,)),
            dma((NJ - 1,)),
            dma((NC,)),
            dma((NC,)),
        ],
        compiler_params=pltpu.CompilerParams(collective_id=1, has_side_effects=True, vmem_limit_bytes=16 * 1024 * 1024),
        name="merge",
    )(stats)


def per_device(
    slab, fetch_rows, w_in, b_in, w_out, query_emb, item_counts, tile_blocks, tile_count, pos_idx
):
    queries, meta, wanted, neg_log, cand = run_tower(
        fetch_rows,
        slab,
        query_emb,
        pos_idx.reshape(QB, 128),
        tile_blocks,
        tile_count.reshape(1, QB),
        item_counts.reshape(NC, 512),
        w_in,
        b_in.reshape(1, H),
        w_out,
    )
    stats, cand = run_score(queries, meta, wanted, neg_log, cand)
    loss = run_merge(stats)
    return (cand[None], loss.reshape(QROWS))


def solution(mesh):
    in_specs = (
        P("catalog", None),
        P("catalog", None, ("query", "dp")),
        P(),
        P(),
        P(),
        P(("query", "dp"), None),
        P("catalog", None, None),
        P(("query", "dp"), "catalog", None),
        P(("query", "dp"), "catalog"),
        P(("query", "dp")),
    )
    out_specs = (P("catalog", None, ("query", "dp"), None), P(("query", "dp")))
    return jax.shard_map(
        per_device, mesh=mesh, in_specs=in_specs, out_specs=out_specs, check_vma=False
    )
```

time: 80.4 us -> 75.3 us (0.937)
  Pallas kernels: 76.6 us -> 72.9 us
  local copies, waits for them, and re-layouts: 2.8 us -> 1.48 us
    pallas_call x1, Pallas kernels: 48.9 us -> 46.1 us  [run_tower(): pl.pallas_call(tower_kernel, out_shape=(jax.ShapeDtypeStruct((NJ, QROWS,...]
    pallas_call x1, Pallas kernels: 13.3 us -> 11.2 us  [run_score(): pl.pallas_call(score_kernel, out_shape=(jax.ShapeDtypeStruct((NJ, 3 * QB,...]
    unnamed x4 -> x3, local copies, waits for them, and re-layouts: 2.8 us -> 1.48 us
    pallas_call x1, Pallas kernels: 14.4 us -> 15.6 us  [run_merge(): pl.pallas_call(merge_kernel, out_shape=jax.ShapeDtypeStruct((QB, 128), jn...]
where the time goes in v3:
time: 75.3 us; the launch traced here: 75.1 us
  Pallas kernels  72.9 us (97%)
  local copies, waits for them, and re-layouts  1.48 us (2%)
    pallas_call x1, Pallas kernels, run_tower(): pl.pallas_call(tower_kernel, out_shape=(jax.ShapeDtypeStruct((NJ, QROWS,...  46.1 us
    pallas_call x1, Pallas kernels, run_merge(): pl.pallas_call(merge_kernel, out_shape=jax.ShapeDtypeStruct((QB, 128), jn...  15.6 us
    pallas_call x1, Pallas kernels, run_score(): pl.pallas_call(score_kernel, out_shape=(jax.ShapeDtypeStruct((NJ, 3 * QB,...  11.2 us

profile of v3, /device:TPU:1, one launch (start us, length us, event | category | flops | bytes accessed | tf_op | source)
XLA Modules:
  0.0 75.1 jit_solution(16497278934805355968)
XLA Ops:
  0.6 46.1 %tower.1 = (bf16[8,1024,512]{2,1,0:T(8,128)(2,1)}, s32[8,16,128]{2,1,0:T(8,128)}, s32[8,8,128]{2,1,0:T(8,128)}, f32[1024,128]{1,0:T(8,128)}, bf16[16,64,512]{2,1,0:T(8,128)(2,1)}) custom-call(s32[1,16,64]{2,1,0:T(8,128)} %fetch.1, bf16[16384,512]{1,0:T(8,128)(2,1)} %slab.1, bf16[1024,512]{1,0:T(8,128)(2,1)} %query.1, s32[8,128]{1,0:T(8,128)} %bitcast.9, ...), custom_call_target="tpu_custom_call" | custom-call | flops 4294967296 | bytes 33554432 | tf_op jit(solution)/shard_map/tower/pallas_call | solution.py:322
  46.7 11.2 %score.1 = (f32[8,24,128]{2,1,0:T(8,128)}, bf16[16,64,512]{2,1,0:T(8,128)(2,1)}) custom-call(bf16[8,1024,512]{2,1,0:T(8,128)(2,1)} %get-tuple-element.9.queries, s32[8,16,128]{2,1,0:T(8,128)} %get-tuple-element.10.meta, s32[8,8,128]{2,1,0:T(8,128)} %get-tuple-element.11.wanted, f32[1024,128]{1,0:T(8,128)} %get-tuple-element.12.neg_log, ...), custom_call_target="tpu_custom_call" | custom-call | flops 536870912 | bytes 10485760 | tf_op jit(solution)/shard_map/score/pallas_call | solution.py:429
  57.9 0.0 copy-start
  58.0 0.9 %copy-done = f32[8,24,128]{2,1,0:T(8,128)S(1)} copy-done((f32[8,24,128]{2,1,0:T(8,128)S(1)}, f32[8,24,128]{2,1,0:T(8,128)}, u32[]{:S(2)}) %copy-start) | copy-done | bytes 98328
  58.8 15.6 %merge.1 = f32[8,128]{1,0:T(8,128)S(1)} custom-call(f32[8,24,128]{2,1,0:T(8,128)S(1)} %copy-done), custom_call_target="tpu_custom_call" | custom-call | tf_op jit(solution)/shard_map/merge/pallas_call | solution.py:527
  74.5 0.6 copy.13
Async XLA Ops:
  57.9 0.9 %copy-start = (f32[8,24,128]{2,1,0:T(8,128)S(1)}, f32[8,24,128]{2,1,0:T(8,128)}, u32[]{:S(2)}) copy-start(f32[8,24,128]{2,1,0:T(8,128)} %get-tuple-element.15.stats) | copy-start | bytes 294916

commit v4 on v3

--- a/solution.py
+++ b/solution.py
@@ -25,7 +25,7 @@
 QB = QROWS // 128
 HALF = QROWS // 2
 SLAB_CHUNK = 1024
-JOBS = 4
+JOBS = 8
 NONE = 256
 LOW = -1e30
 VMEM_LIMIT = 60 * 1024 * 1024

time: 75.3 us -> 73.8 us (0.980)
  Pallas kernels: 72.9 us -> 71.4 us
    pallas_call x1, Pallas kernels: 11.2 us -> 10.1 us  [run_score(): pl.pallas_call(score_kernel, out_shape=(jax.ShapeDtypeStruct((NJ, 3 * QB,...]
where the time goes in v4:
time: 73.8 us; the launch traced here: 73.5 us
  Pallas kernels  71.4 us (97%)
  local copies, waits for them, and re-layouts  1.48 us (2%)
    pallas_call x1, Pallas kernels, run_tower(): pl.pallas_call(tower_kernel, out_shape=(jax.ShapeDtypeStruct((NJ, QROWS,...  46.1 us
    pallas_call x1, Pallas kernels, run_merge(): pl.pallas_call(merge_kernel, out_shape=jax.ShapeDtypeStruct((QB, 128), jn...  15.2 us
    pallas_call x1, Pallas kernels, run_score(): pl.pallas_call(score_kernel, out_shape=(jax.ShapeDtypeStruct((NJ, 3 * QB,...  10.1 us
    unnamed x3, local copies, waits for them, and re-layouts  1.48 us

profile of v4, /device:TPU:1, one launch (start us, length us, event | category | flops | bytes accessed | tf_op | source)
XLA Modules:
  0.0 73.5 jit_solution(14267180961286502576)
XLA Ops:
  0.6 46.1 %tower.1 = (bf16[8,1024,512]{2,1,0:T(8,128)(2,1)}, s32[8,16,128]{2,1,0:T(8,128)}, s32[8,8,128]{2,1,0:T(8,128)}, f32[1024,128]{1,0:T(8,128)}, bf16[16,64,512]{2,1,0:T(8,128)(2,1)}) custom-call(s32[1,16,64]{2,1,0:T(8,128)} %fetch.1, bf16[16384,512]{1,0:T(8,128)(2,1)} %slab.1, bf16[1024,512]{1,0:T(8,128)(2,1)} %query.1, s32[8,128]{1,0:T(8,128)} %bitcast.9, ...), custom_call_target="tpu_custom_call" | custom-call | flops 4294967296 | bytes 33554432 | tf_op jit(solution)/shard_map/tower/pallas_call | solution.py:322
  46.7 10.1 %score.1 = (f32[8,24,128]{2,1,0:T(8,128)}, bf16[16,64,512]{2,1,0:T(8,128)(2,1)}) custom-call(bf16[8,1024,512]{2,1,0:T(8,128)(2,1)} %get-tuple-element.9.queries, s32[8,16,128]{2,1,0:T(8,128)} %get-tuple-element.10.meta, s32[8,8,128]{2,1,0:T(8,128)} %get-tuple-element.11.wanted, f32[1024,128]{1,0:T(8,128)} %get-tuple-element.12.neg_log, ...), custom_call_target="tpu_custom_call" | custom-call | flops 536870912 | bytes 10485760 | tf_op jit(solution)/shard_map/score/pallas_call | solution.py:429
  56.8 0.0 copy-start
  56.8 0.9 %copy-done = f32[8,24,128]{2,1,0:T(8,128)S(1)} copy-done((f32[8,24,128]{2,1,0:T(8,128)S(1)}, f32[8,24,128]{2,1,0:T(8,128)}, u32[]{:S(2)}) %copy-start) | copy-done | bytes 98328
  57.7 15.2 %merge.1 = f32[8,128]{1,0:T(8,128)S(1)} custom-call(f32[8,24,128]{2,1,0:T(8,128)S(1)} %copy-done), custom_call_target="tpu_custom_call" | custom-call | tf_op jit(solution)/shard_map/merge/pallas_call | solution.py:527
  72.9 0.6 copy.13
Async XLA Ops:
  56.8 0.9 %copy-start = (f32[8,24,128]{2,1,0:T(8,128)S(1)}, f32[8,24,128]{2,1,0:T(8,128)}, u32[]{:S(2)}) copy-start(f32[8,24,128]{2,1,0:T(8,128)} %get-tuple-element.15.stats) | copy-start | bytes 294916

commit v5 on v4

--- a/solution.py
+++ b/solution.py
@@ -25,7 +25,7 @@
 QB = QROWS // 128
 HALF = QROWS // 2
 SLAB_CHUNK = 1024
-JOBS = 8
+JOBS = 16
 NONE = 256
 LOW = -1e30
 VMEM_LIMIT = 60 * 1024 * 1024
@@ -48,7 +48,6 @@
     }
 for _n in (0, 128):
     FLOWS |= {
-        f"y{_n + 256}": ("y", (0, 0), _n + 256, 128, None),
         f"r{_n + 256}": ("r", (0, 0), _n + 256, 128, None),
         f"l{_n}": ("l", (0, 0), _n, 128, None),
     }
@@ -63,6 +62,8 @@
         f"lly{_n}": ("y", (2, 0), _n + 256, 128, f"ll{_n + 256}"),
     }
 FLOWS |= {
+    "ys": ("y", (0, 0), "own", 128, None),
+    "w": ("w", (0, 1), "other", 128, "ys"),
     "yrr": ("r", (-1, 1), 0, 128, "yr0"),
     "yll": ("l", (1, 1), 128, 128, "yl128"),
 }
@@ -108,6 +109,7 @@
         "r": {"catalog": t, "query": right, "dp": d},
         "l": {"catalog": t, "query": left, "dp": d},
         "y": {"catalog": flip(t, 8, 4), "query": x, "dp": 1 - d},
+        "w": {"catalog": flip(t, 8, 4), "query": x, "dp": d},
     }
     sibling = {"catalog": flip(t, 1, 4), "query": x, "dp": d}
 
@@ -139,10 +141,15 @@
         xo = (x + ox + NX) % NX
         return xo * ND + (1 - d if oy else d)
 
+    y_lo = t // 8
+
+    def first_row(first):
+        return {"own": 256 + 128 * y_lo, "other": 384 - 128 * y_lo}.get(first, first)
+
     def flow_copy(name):
         hop, place, first, count, _ = FLOWS[name]
         jo = origin(place)
-        rows = pl.ds(pl.multiple_of(core * HALF + first, 128), count)
+        rows = pl.ds(pl.multiple_of(core * HALF + first_row(first), 128), count)
         src = query.at[rows] if place == (0, 0) else queries.at[jo, rows]
         return pltpu.make_async_remote_copy(
             src_ref=src,
@@ -155,6 +162,7 @@
 
     def core_copy(name):
         _, _, first, count, _ = FLOWS[name]
+        first = first_row({"own": "other", "other": "own"}.get(first, first))
         part = queries.at[origin(landed(name)), pl.ds(pl.multiple_of(core * HALF + first, 128), count)]
         return pltpu.make_async_remote_copy(
             src_ref=part,
@@ -246,11 +254,11 @@
         if k == 12:
             advance("y128", "r128", "l384")
         if k == 6:
-            advance("r256", "l0", "y256")
+            advance("r256", "l0", "ys")
         if k:
             a2a_copy(k).start()
 
-    advance("rr0", "ll256", "yr0", "yl0", "r384", "l128", "y384")
+    advance("rr0", "ll256", "yr0", "yl0", "r384", "l128", "w")
     w_in_copy.wait()
     w_out_copy.wait()
 

time: 73.8 us -> 72.8 us (0.986)
  Pallas kernels: 71.4 us -> 70.1 us
    pallas_call x1, Pallas kernels: 10.1 us -> 8.22 us  [run_score(): pl.pallas_call(score_kernel, out_shape=(jax.ShapeDtypeStruct((NJ, 3 * QB,...]
where the time goes in v5:
time: 72.8 us; the launch traced here: 72.3 us
  Pallas kernels  70.1 us (96%)
  local copies, waits for them, and re-layouts  1.48 us (2%)
    pallas_call x1, Pallas kernels, run_tower(): pl.pallas_call(tower_kernel, out_shape=(jax.ShapeDtypeStruct((NJ, QROWS,...  46.1 us
    pallas_call x1, Pallas kernels, run_merge(): pl.pallas_call(merge_kernel, out_shape=jax.ShapeDtypeStruct((QB, 128), jn...  15.8 us
    pallas_call x1, Pallas kernels, run_score(): pl.pallas_call(score_kernel, out_shape=(jax.ShapeDtypeStruct((NJ, 3 * QB,...  8.22 us
    unnamed x3, local copies, waits for them, and re-layouts  1.48 us

profile of v5, /device:TPU:1, one launch (start us, length us, event | category | flops | bytes accessed | tf_op | source)
XLA Modules:
  0.0 72.3 jit_solution(9089300873518797812)
XLA Ops:
  0.6 46.1 %tower.1 = (bf16[8,1024,512]{2,1,0:T(8,128)(2,1)}, s32[8,16,128]{2,1,0:T(8,128)}, s32[8,8,128]{2,1,0:T(8,128)}, f32[1024,128]{1,0:T(8,128)}, bf16[16,64,512]{2,1,0:T(8,128)(2,1)}) custom-call(s32[1,16,64]{2,1,0:T(8,128)} %fetch.1, bf16[16384,512]{1,0:T(8,128)(2,1)} %slab.1, bf16[1024,512]{1,0:T(8,128)(2,1)} %query.1, s32[8,128]{1,0:T(8,128)} %bitcast.9, ...), custom_call_target="tpu_custom_call" | custom-call | flops 4294967296 | bytes 33554432 | tf_op jit(solution)/shard_map/tower/pallas_call | solution.py:330
  46.7 8.2 %score.1 = (f32[8,24,128]{2,1,0:T(8,128)}, bf16[16,64,512]{2,1,0:T(8,128)(2,1)}) custom-call(bf16[8,1024,512]{2,1,0:T(8,128)(2,1)} %get-tuple-element.9.queries, s32[8,16,128]{2,1,0:T(8,128)} %get-tuple-element.10.meta, s32[8,8,128]{2,1,0:T(8,128)} %get-tuple-element.11.wanted, f32[1024,128]{1,0:T(8,128)} %get-tuple-element.12.neg_log, ...), custom_call_target="tpu_custom_call" | custom-call | flops 536870912 | bytes 10485760 | tf_op jit(solution)/shard_map/score/pallas_call | solution.py:437
  54.9 0.0 copy-start
  55.0 0.9 %copy-done = f32[8,24,128]{2,1,0:T(8,128)S(1)} copy-done((f32[8,24,128]{2,1,0:T(8,128)S(1)}, f32[8,24,128]{2,1,0:T(8,128)}, u32[]{:S(2)}) %copy-start) | copy-done | bytes 98328
  55.8 15.8 %merge.1 = f32[8,128]{1,0:T(8,128)S(1)} custom-call(f32[8,24,128]{2,1,0:T(8,128)S(1)} %copy-done), custom_call_target="tpu_custom_call" | custom-call | tf_op jit(solution)/shard_map/merge/pallas_call | solution.py:535
  71.7 0.6 copy.13
Async XLA Ops:
  54.9 0.9 %copy-start = (f32[8,24,128]{2,1,0:T(8,128)S(1)}, f32[8,24,128]{2,1,0:T(8,128)}, u32[]{:S(2)}) copy-start(f32[8,24,128]{2,1,0:T(8,128)} %get-tuple-element.15.stats) | copy-start | bytes 294916
